TPU v7x, 32 devices: a whole 2x2x4 slice. The times are simulated.
32 devices in a mesh: ctx: 8 (over z, x), tp: 2 (over core), ep: 2 (over y).
Axes of the slice: x: 2, y: 2, z: 4, core: 2. Of those that a mesh axis runs over, the one named last changes fastest.
Arguments:
- hidden: bfloat16 [1024, 3584], P('ctx'), may hold values from -40 to 40
- grad_out: bfloat16 [1024, 3584], P('ctx'), may hold values from -6 to 6
- gain: float32 [3584], replicated, may hold values from 0.5 to 1.5
- dense_gate: bfloat16 [2432, 3584], P(('tp', 'ep')), may hold values from -0.09375 to 0.09375
- dense_up: bfloat16 [2432, 3584], P(('tp', 'ep')), may hold values from -0.09375 to 0.09375
- dense_down: bfloat16 [2432, 3584], P(('tp', 'ep')), may hold values from -0.125 to 0.125
- expert_gate: bfloat16 [8, 3840, 3584], P('ctx', ('tp', 'ep')), may hold values from -0.09375 to 0.09375
- expert_up: bfloat16 [8, 3840, 3584], P('ctx', ('tp', 'ep')), may hold values from -0.09375 to 0.09375
- expert_down: bfloat16 [8, 3840, 3584], P('ctx', ('tp', 'ep')), may hold values from -0.09375 to 0.09375
- out_proj: bfloat16 [1024, 3584], P(('tp', 'ep')), may hold values from -0.1875 to 0.1875
- queries: bfloat16 [1024, 1024], P('ctx', ('tp', 'ep')), may hold values from -12 to 12
- keys: bfloat16 [1024, 1024], P('ctx', ('tp', 'ep')), may hold values from -12 to 12
- values: bfloat16 [1024, 1024], P('ctx', ('tp', 'ep')), may hold values from -6 to 6
- route_ids: int32 [1024, 2], P('ctx'), may hold values from 0 to 7, all different within a row; in each aligned block of 128 rows (0 to 127, 128 to 255, ...) at most 40 rows name the same one
- route_weights: float32 [1024, 2], P('ctx'), may hold values from 0.2 to 1
Outputs:
- grad_hidden: bfloat16 [1024, 3584], P('ctx')
- grad_queries: bfloat16 [1024, 1024], P('ctx', ('tp', 'ep'))
- grad_keys: bfloat16 [1024, 1024], P('ctx', ('tp', 'ep'))
- grad_values: bfloat16 [1024, 1024], P('ctx', ('tp', 'ep'))
Inputs may be any that keep to these rules, and one draw needn't show every extreme that they name: `route_ids`: the two ids of a token differ. In each aligned block of 128 tokens no expert is named by more than 40 routed rows, a bound that some block reaches.
All inputs are finite; a program needn't handle non-finite values.
Results may differ from a plain program's by a relative error of at most 0.03.
Values may be sent and summed in bfloat16 or wider, within the bound.
A program may use at most 128 MiB of HBM per device.

v0:
```python
import jax
import jax.numpy as jnp
from jax import lax
from jax.sharding import PartitionSpec as P

HEAD_DIM = 128


NEG_FILL = -1e30
EPSILON = 1e-05


def shifted(shard, axis, by):
    devices = lax.axis_size(axis)
    return lax.ppermute(shard, axis, [(i, (i + by) % devices) for i in range(devices)])


def contract_last(left_rows, right_rows):
    return lax.dot_general(
        left_rows, right_rows, (((1,), (1,)), ((), ())), preferred_element_type=jnp.float32
    )


def swiglu_grad(inputs, upstream, w_gate, w_up, w_down):
    gate_pre = contract_last(inputs, w_gate)
    up_pre = contract_last(inputs, w_up)
    back_grad = contract_last(upstream, w_down)
    sigmoid_gate = jax.nn.sigmoid(gate_pre)
    grad_gate = (
        back_grad * up_pre * sigmoid_gate * (1.0 + gate_pre * (1.0 - sigmoid_gate))
    ).astype(jnp.bfloat16)
    grad_upper = (back_grad * gate_pre * sigmoid_gate).astype(jnp.bfloat16)
    return jnp.dot(grad_gate, w_gate, preferred_element_type=jnp.float32) + jnp.dot(
        grad_upper, w_up, preferred_element_type=jnp.float32
    )


def head_scores(left_heads, right_heads):
    return jnp.einsum("qhd,khd->hqk", left_heads, right_heads, preferred_element_type=jnp.float32)


def forward_piece(running, pieces, query_heads, upstream_heads, query_pos):
    run_max, run_sum, run_dot = running
    key_count = pieces[0].shape[0]
    key_heads = pieces[0].reshape(key_count, -1, HEAD_DIM)
    value_heads = pieces[1].reshape(key_count, -1, HEAD_DIM)
    key_pos = lax.iota(jnp.int32, key_count)
    allowed = key_pos[None, None, :] <= query_pos[None, :, None]
    scores = jnp.where(allowed, head_scores(query_heads, key_heads) * HEAD_DIM ** (-0.5), NEG_FILL)
    new_max = jnp.maximum(run_max, jnp.max(scores, axis=2))
    weights = jnp.where(allowed, jnp.exp(scores - new_max[:, :, None]), 0.0)
    grad_probs = head_scores(upstream_heads, value_heads)
    return (new_max, jnp.sum(weights, axis=2), jnp.sum(weights * grad_probs, axis=2))


def backward_terms(
    query_heads, upstream_heads, key_heads, value_heads, log_norm, delta_row, allowed
):
    score_scale = HEAD_DIM ** (-0.5)
    scores = head_scores(query_heads, key_heads) * score_scale
    probs = jnp.where(allowed, jnp.exp(scores - log_norm[:, :, None]), 0.0)
    grad_scores = probs * (head_scores(upstream_heads, value_heads) - delta_row[:, :, None])
    probs_half = probs.astype(jnp.bfloat16)
    grad_half = grad_scores.astype(jnp.bfloat16)
    grad_values = jnp.einsum(
        "hqk,qhd->khd", probs_half, upstream_heads, preferred_element_type=jnp.float32
    )
    grad_keys = (
        jnp.einsum("hqk,qhd->khd", grad_half, query_heads, preferred_element_type=jnp.float32)
        * score_scale
    )
    grad_queries = (
        jnp.einsum("hqk,khd->qhd", grad_half, key_heads, preferred_element_type=jnp.float32)
        * score_scale
    )
    return (grad_queries, grad_keys, grad_values)


def body(
    hidden,
    grad_out,
    gain,
    dense_gate,
    dense_up,
    dense_down,
    expert_gate,
    expert_up,
    expert_down,
    out_proj,
    queries,
    keys,
    values,
    route_ids,
    route_weights,
):
    row_count = hidden.shape[0]
    feat_width = hidden.shape[1]
    pick_count = route_ids.shape[1]
    hidden_f = hidden.astype(jnp.float32)
    inverse = lax.rsqrt(jnp.mean(hidden_f * hidden_f, axis=1, keepdims=True) + EPSILON)
    normed = hidden_f * inverse
    mixed_in = (normed * gain).astype(jnp.bfloat16)
    dense_part = swiglu_grad(mixed_in, grad_out, dense_gate, dense_up, dense_down)
    expert_count = lax.axis_size("ctx")
    capacity = 5 * row_count // (2 * expert_count)
    flat_ids = route_ids.reshape(-1)
    hits = (flat_ids[:, None] == lax.iota(jnp.int32, expert_count)[None, :]).astype(jnp.int32)
    earlier = jnp.cumsum(hits, axis=0) - hits
    slots = jnp.sum(earlier * hits, axis=1)
    places = flat_ids * capacity + slots
    owners = lax.iota(jnp.int32, pick_count * row_count) // pick_count
    token_of = jnp.full((expert_count * capacity,), row_count, jnp.int32).at[places].set(owners)
    weight_of = (
        jnp.zeros((expert_count * capacity,), jnp.float32).at[places].set(route_weights.reshape(-1))
    )
    present = token_of < row_count
    picked = jnp.minimum(token_of, row_count - 1)
    send_in = jnp.where(present[:, None], mixed_in[picked], jnp.zeros((), jnp.bfloat16)).reshape(
        expert_count, capacity, feat_width
    )
    send_grad = (
        (grad_out[picked].astype(jnp.float32) * weight_of[:, None])
        .astype(jnp.bfloat16)
        .reshape(expert_count, capacity, feat_width)
    )
    inputs = lax.all_to_all(send_in, "ctx", split_axis=0, concat_axis=0, tiled=True)
    upstream = lax.all_to_all(send_grad, "ctx", split_axis=0, concat_axis=0, tiled=True)
    slot_count = inputs.shape[1]
    partial_value = swiglu_grad(
        inputs.reshape(-1, feat_width),
        upstream.reshape(-1, feat_width),
        expert_gate[0],
        expert_up[0],
        expert_down[0],
    )
    partial_value = partial_value.reshape(expert_count, slot_count, feat_width)
    partial_value = lax.psum(partial_value, ("tp", "ep"))
    returned = lax.all_to_all(partial_value, "ctx", split_axis=0, concat_axis=0, tiled=True)
    routed = (
        returned.reshape(expert_count * capacity, feat_width)[places]
        .reshape(row_count, pick_count, feat_width)
        .sum(axis=1)
    )
    total_grad = lax.psum(dense_part, ("tp", "ep")) + routed
    scaled_grad = total_grad * gain
    grad_hidden = (
        grad_out.astype(jnp.float32)
        + inverse * (scaled_grad - normed * jnp.mean(scaled_grad * normed, axis=1, keepdims=True))
    ).astype(jnp.bfloat16)
    grad_heads = contract_last(grad_hidden, out_proj).astype(jnp.bfloat16)
    head_width = queries.shape[1]
    query_heads = queries.reshape(row_count, -1, HEAD_DIM)
    upstream_heads = grad_heads.reshape(row_count, -1, HEAD_DIM)
    heads_here = query_heads.shape[1]
    my_block = lax.axis_index("ctx")
    block_count = lax.axis_size("ctx")
    query_pos = my_block * row_count + lax.iota(jnp.int32, row_count)
    start_state = (
        jnp.full((heads_here, row_count), NEG_FILL, jnp.float32),
        jnp.zeros((heads_here, row_count), jnp.float32),
        jnp.zeros((heads_here, row_count), jnp.float32),
    )
    run_max, run_sum, run_dot = forward_piece(
        start_state,
        (
            lax.all_gather(keys, "ctx", axis=0, tiled=True),
            lax.all_gather(values, "ctx", axis=0, tiled=True),
        ),
        query_heads,
        upstream_heads,
        query_pos,
    )
    log_norm = run_max + jnp.log(run_sum)
    delta_row = run_dot / run_sum

    def cycle_visit(cycle_state, hop_index):
        keys_now, values_now, sum_keys, sum_values, sum_queries = cycle_state
        held_block = (my_block + hop_index) % block_count
        key_pos = held_block * row_count + lax.iota(jnp.int32, row_count)
        allowed = key_pos[None, None, :] <= query_pos[None, :, None]
        term_queries, term_keys, term_values = backward_terms(
            query_heads,
            upstream_heads,
            keys_now.reshape(row_count, -1, HEAD_DIM),
            values_now.reshape(row_count, -1, HEAD_DIM),
            log_norm,
            delta_row,
            allowed,
        )
        sum_keys, sum_values = shifted(
            (
                sum_keys + term_keys.reshape(row_count, head_width),
                sum_values + term_values.reshape(row_count, head_width),
            ),
            "ctx",
            -1,
        )
        return (
            keys_now,
            values_now,
            sum_keys,
            sum_values,
            sum_queries + term_queries.reshape(row_count, head_width),
        )

    def cycle_loop(hop_index, cycle_state):
        cycle_state = cycle_visit(cycle_state, hop_index)
        keys_next, values_next = shifted((cycle_state[0], cycle_state[1]), "ctx", -1)
        return (keys_next, values_next, cycle_state[2], cycle_state[3], cycle_state[4])

    zero_heads = jnp.zeros((row_count, head_width), jnp.float32)
    cycle_state = lax.fori_loop(
        0, block_count - 1, cycle_loop, (keys, values, zero_heads, zero_heads, zero_heads)
    )
    cycle_state = cycle_visit(cycle_state, block_count - 1)
    return (
        grad_hidden,
        cycle_state[4].astype(jnp.bfloat16),
        cycle_state[2].astype(jnp.bfloat16),
        cycle_state[3].astype(jnp.bfloat16),
    )


def solution(mesh):
    return jax.shard_map(
        body,
        mesh=mesh,
        in_specs=(
            P("ctx", None),
            P("ctx", None),
            P(),
            P(("tp", "ep"), None),
            P(("tp", "ep"), None),
            P(("tp", "ep"), None),
            P("ctx", ("tp", "ep"), None),
            P("ctx", ("tp", "ep"), None),
            P("ctx", ("tp", "ep"), None),
            P(("tp", "ep"), None),
            P("ctx", ("tp", "ep")),
            P("ctx", ("tp", "ep")),
            P("ctx", ("tp", "ep")),
            P("ctx", None),
            P("ctx", None),
        ),
        out_specs=(
            P("ctx", None),
            P("ctx", ("tp", "ep")),
            P("ctx", ("tp", "ep")),
            P("ctx", ("tp", "ep")),
        ),
        check_vma=False,
    )
```

profile of v0, /device:TPU:0, one launch (start us, length us, event | category | flops | bytes accessed | tf_op | source)
XLA Modules:
  0.0 580.8 jit_solution(11002946243216162531)
XLA Ops:
  15.6 3.7 gather_fusion.1
  19.3 3.3 broadcast_select_fusion
  22.6 7.3 %all-to-all-start.1 = ((bf16[8,40,3584]{2,1,0:T(8,128)(2,1)}), bf16[8,40,3584]{2,1,0:T(8,128)(2,1)}, u32[]{:S(2)}, u32[]{:S(2)}) async-start(bf16[8,40,3584]{2,1,0:T(8,128)(2,1)} %broadcast_select_fusion), calls=%async_computation.1 | async-start | bytes 4587520 | tf_op jit(solution)/shard_map/all_to_all | solution.py:126
  29.8 8.8 %gather_fusion = bf16[320,3584]{1,0:T(8,128)(2,1)} fusion(bf16[128,3584]{1,0:T(8,128)(2,1)} %param.18, s32[1024]{0:T(1024)S(1)} %pad_clamp_fusion.1), kind=kCustom, calls=%fused_computation | custom fusion | bytes 4588800 | tf_op jit(solution)/shard_map/gather | solution.py:122
  40.4 3.6 fusion.26
  43.9 38.5 %all-to-all-done.1 = bf16[8,40,3584]{2,1,0:T(8,128)(2,1)} async-done(((bf16[8,40,3584]{2,1,0:T(8,128)(2,1)}), bf16[8,40,3584]{2,1,0:T(8,128)(2,1)}, u32[]{:S(2)}, u32[]{:S(2)}) %all-to-all-start.1) | async-done | bytes 2293792 | tf_op jit(solution)/shard_map/all_to_all | solution.py:126
  82.4 4.4 all-to-all-start
  87.0 3.6 fusion.89
  90.6 4.2 fusion.88
  94.9 8.4 %fusion.61 = f32[128,3584]{1,0:T(8,128)} fusion(bf16[608,3584]{1,0:T(8,128)(2,1)} %param.20, f32[128,608]{0,1:T(8,128)} %fusion.88, bf16[128,3584]{1,0:T(8,128)(2,1)S(1)} %fusion.30, bf16[608,3584]{1,0:T(8,128)(2,1)} %param.21, f32[128,608]{0,1:T(8,128)S(1)} %fusion.89), kind=kOutput, calls=%fused_computation.82 | convolution fusion | flops 1116463104 | bytes 12091392 | tf_op jit(solution)/shard_map/dot_general | solution.py:33
  103.3 5.1 convolution_add_fusion
  108.4 7.3 %fusion.15 = f32[320,960]{1,0:T(8,128)} fusion(bf16[320,3584]{1,0:T(8,128)(2,1)} %bitcast.8, bf16[1,960,3584]{2,1,0:T(8,128)(2,1)} %param.23), kind=kOutput, calls=%fused_computation.29 | convolution fusion | flops 2202009600 | bytes 10403840 | tf_op jit(solution)/shard_map/dot_general | solution.py:19
  115.6 23.2 %all-to-all-done = bf16[8,40,3584]{2,1,0:T(8,128)(2,1)} async-done(((bf16[8,40,3584]{2,1,0:T(8,128)(2,1)}), bf16[8,40,3584]{2,1,0:T(8,128)(2,1)}, u32[]{:S(2)}, u32[]{:S(2)}) %all-to-all-start) | async-done | bytes 2293792 | tf_op jit(solution)/shard_map/all_to_all | solution.py:127
  138.8 7.3 %fusion.21 = f32[320,960]{1,0:T(8,128)} fusion(bf16[320,3584]{1,0:T(8,128)(2,1)} %bitcast.5, bf16[1,960,3584]{2,1,0:T(8,128)(2,1)} %param.25), kind=kOutput, calls=%fused_computation.35 | convolution fusion | flops 2202009600 | bytes 10403840 | tf_op jit(solution)/shard_map/dot_general | solution.py:19
  146.1 13.5 %fusion.13 = f32[320,3584]{1,0:T(8,128)} fusion(bf16[1,960,3584]{2,1,0:T(8,128)(2,1)} %param.23, f32[320,960]{1,0:T(8,128)} %fusion.21, bf16[320,3584]{1,0:T(8,128)(2,1)} %bitcast.8, bf16[1,960,3584]{2,1,0:T(8,128)(2,1)} %param.24, f32[320,960]{1,0:T(8,128)} %fusion.15), kind=kOutput, calls=%fused_computation.27 | convolution fusion | flops 4407091200 | bytes 23101440 | tf_op jit(solution)/shard_map/dot_general | solution.py:33
  159.5 10.0 %fusion.23 = f32[320,3584]{1,0:T(8,128)} fusion(f32[320,3584]{1,0:T(8,128)} %fusion.13, bf16[1,960,3584]{2,1,0:T(8,128)(2,1)} %param.24, f32[320,960]{1,0:T(8,128)} %fusion.21, f32[320,960]{1,0:T(8,128)} %fusion.15), kind=kOutput, calls=%fused_computation.37 | convolution fusion | flops 2204999680 | bytes 18513920 | tf_op jit(solution)/shard_map/dot_general | solution.py:33
  169.6 121.1 %all-reduce.3.cloned.1.call-done = (f32[128,3584]{1,0:T(8,128)}, f32[8,40,3584]{2,1,0:T(8,128)}) async-done(((f32[128,3584]{1,0:T(8,128)}, f32[8,40,3584]{2,1,0:T(8,128)}), (f32[128,3584]{1,0:T(8,128)}, f32[8,40,3584]{2,1,0:T(8,128)})) %all-reduce.3.cloned.1.call-update) | async-done | bytes 6422544 | tf_op jit(solution)/shard_map/psum | solution.py:144
  290.7 5.6 all-to-all-start.2
  296.9 121.9 %all_gather.6 = bf16[1024,256]{0,1:T(8,128)(2,1)S(1)} all-gather(bf16[128,256]{0,1:T(8,128)(2,1)S(1)} %copy.63), channel_id=1, replica_groups=mesh['ctx'=8,'tp'=2,'ep'=2] {'ctx'}, dimensions={0}, use_global_device_ids=true | all-gather | bytes 589824 | tf_op jit(solution)/shard_map/all_gather | solution.py:166
  420.7 28.9 %all_gather.7 = bf16[1024,256]{0,1:T(8,128)(2,1)} all-gather(bf16[128,256]{0,1:T(8,128)(2,1)S(1)} %copy.60), channel_id=1, replica_groups=mesh['ctx'=8,'tp'=2,'ep'=2] {'ctx'}, dimensions={0}, use_global_device_ids=true | all-gather | bytes 589824 | tf_op jit(solution)/shard_map/all_gather | solution.py:167
  449.6 7.5 %gather_fusion.2 = f32[256,3584]{1,0:T(8,128)} fusion(f32[320,3584]{1,0:T(8,128)} %bitcast.12, s32[1024]{0:T(1024)S(1)} %pad_clamp_fusion), kind=kCustom, calls=%fused_computation.2 | custom fusion | bytes 7341056 | tf_op jit(solution)/shard_map/gather | solution.py:140
  457.1 5.6 reshape.303
  462.6 7.8 %reduce_sum.59 = f32[128,3584]{1,0:T(8,128)} reduce(f32[128,2,3584]{2,1,0:T(2,128)} %reshape.303, f32[]{:T(128)} %constant.124.clone.1), dimensions={1}, to_apply=%region_8.9 | reduce | flops 458752 | bytes 5505028 | tf_op jit(solution)/shard_map/reduce_sum | solution.py:142
  470.4 2.7 fusion.31
  476.6 1.8 fusion.50
  478.4 85.5 %while.24 = (s32[]{:T(128)}, bf16[128,256]{0,1:T(8,128)(2,1)S(1)}, bf16[128,256]{1,0:T(8,128)(2,1)S(1)}, f32[128,256]{0,1:T(8,128)S(1)}, f32[128,256]{0,1:T(8,12...) while((s32[]{:T(128)}, bf16[128,256]{0,1:T(8,128)(2,1)S(1)}, ...), condition=%wide.region_14.15_spmd.clone, body=%wide.region_13.14_spmd.clone.sunk | while | flops 42385680 | bytes 5018068 | solution.py:212
  478.5 2.7 collective-permute-start.1
  482.4 2.7 collective-permute-start.3
  485.4 3.0 collective-permute-done.2
  489.7 4.0 collective-permute-start
  496.7 2.0 collective-permute-done.1
  498.6 2.8 collective-permute-done.2
  501.4 1.7 collective-permute-done.3
  503.1 4.0 collective-permute-start
  509.7 2.4 collective-permute-done.1
  512.2 2.5 collective-permute-done.2
  516.1 4.0 collective-permute-start
  522.6 2.5 collective-permute-done.1
  528.0 4.0 collective-permute-start
  534.8 1.8 collective-permute-done.1
  539.5 3.6 collective-permute-start
  544.1 2.7 collective-permute-start.2
  547.5 1.9 collective-permute-done.2
  549.4 2.9 collective-permute-done.3
  552.3 4.2 collective-permute-start
  560.7 1.7 collective-permute-done.2
  565.0 3.1 collective-permute-start.5
  570.2 2.4 collective-permute-done.4
  (233 shorter events, 48.3 us)
Async XLA Ops:
  7.2 468.4 %copy-start = (bf16[256,3584]{1,0:T(8,128)(2,1)S(1)}, bf16[256,3584]{1,0:T(8,128)(2,1)}, u32[]{:S(2)}) copy-start(bf16[256,3584]{1,0:T(8,128)(2,1)} %param.26) | copy-start | bytes 5505028
  22.6 59.8 %all-to-all-start.1 = ((bf16[8,40,3584]{2,1,0:T(8,128)(2,1)}), bf16[8,40,3584]{2,1,0:T(8,128)(2,1)}, u32[]{:S(2)}, u32[]{:S(2)}) async-start(bf16[8,40,3584]{2,1,0:T(8,128)(2,1)} %broadcast_select_fusion), calls=%async_computation.1 | async-start | bytes 4587520 | tf_op jit(solution)/shard_map/all_to_all | solution.py:126
  29.8 8.8 %copy-start.12 = (f32[128,2]{0,1:T(2,128)S(1)}, f32[128,2]{0,1:T(2,128)}, u32[]{:S(2)}) copy-start(f32[128,2]{0,1:T(2,128)} %param.31) | copy-start | bytes 3076
  82.4 56.4 %all-to-all-start = ((bf16[8,40,3584]{2,1,0:T(8,128)(2,1)}), bf16[8,40,3584]{2,1,0:T(8,128)(2,1)}, u32[]{:S(2)}, u32[]{:S(2)}) async-start(bf16[8,40,3584]{2,1,0:T(8,128)(2,1)} %fusion.26), calls=%async_computation | async-start | bytes 4587520 | tf_op jit(solution)/shard_map/all_to_all | solution.py:127
  86.8 203.9 %all-reduce.3.cloned.1.call-start = ((), (), s32[]{:S(2)}) async-start(), calls=%async_computation.3 | async-start | bytes 12845056 | tf_op jit(solution)/shard_map/psum | solution.py:144
  87.0 3.6 copy-start.1
  290.7 5.6 copy-start.10
  290.7 5.8 copy-start.11
  290.7 158.9 %all-to-all-start.2 = ((f32[8,40,3584]{2,1,0:T(8,128)}), f32[8,40,3584]{2,1,0:T(8,128)}, u32[]{:S(2)}, u32[]{:S(2)}) async-start(f32[8,40,3584]{2,1,0:T(8,128)} %get-tuple-element.395), calls=%async_computation.2 | async-start | bytes 9175040 | tf_op jit(solution)/shard_map/all_to_all | solution.py:138
  419.3 1.0 copy-start.6
  462.6 7.8 %copy-start.4 = (bf16[128,3584]{1,0:T(8,128)(2,1)S(1)}, bf16[128,3584]{1,0:T(8,128)(2,1)}, u32[]{:S(2)}) copy-start(bf16[128,3584]{1,0:T(8,128)(2,1)} %param.17) | copy-start | bytes 2752516
  462.6 7.8 %copy-start.9 = (f32[3584]{0:T(1024)S(1)}, f32[3584]{0:T(1024)}, u32[]{:S(2)}) copy-start(f32[3584]{0:T(1024)} %param.19) | copy-start | bytes 43012
  470.4 2.7 copy-start.2
  470.4 2.9 copy-start.3
  470.4 3.4 copy-start.5
  474.6 0.9 copy-start.7
  475.5 1.0 copy-start.8
  478.4 7.0 %collective-permute-start = (bf16[128,256]{0,1:T(8,128)(2,1)S(1)}, bf16[128,256]{0,1:T(8,128)(2,1)S(1)}, u32[]{:S(2)}, u32[]{:S(2)}) collective-permute-start(bf16[128,256]{0,1:T(8,128)(2,1)S(1)} %copy.122), channel_id=1, source_target_pairs={{0,28},{4,0},{8,4},{12,8},{16,12},{20,16},{24,20},{28,24},{1,29},{... | collective-permute-start | bytes 196616 | tf_op jit(solution)/shard_map/while/body/eval_jaxpr/ppermute | solution.py:15
  478.5 6.9 %collective-permute-start.1 = (bf16[128,256]{1,0:T(8,128)(2,1)S(1)}, bf16[128,256]{1,0:T(8,128)(2,1)S(1)}, u32[]{:S(2)}, u32[]{:S(2)}) collective-permute-start(bf16[128,256]{1,0:T(8,128)(2,1)S(1)} %copy.123), channel_id=1, source_target_pairs={{0,28},{4,0},{8,4},{12,8},{16,12},{20,16},{24,20},{28,24},{1,29},{... | collective-permute-start | bytes 196616 | tf_op jit(solution)/shard_map/while/body/eval_jaxpr/ppermute | solution.py:15
  482.1 6.3 %collective-permute-start.2 = (f32[128,256]{0,1:T(8,128)S(1)}, f32[128,256]{0,1:T(8,128)S(1)}, u32[]{:S(2)}, u32[]{:S(2)}) collective-permute-start(f32[128,256]{0,1:T(8,128)S(1)} %bitcast_add_fusion.7), channel_id=1, source_target_pairs={{0,28},{4,0},{8,4},{12,8},{16,12},{20,16},{24,20},{28,24},{1,29},{... | collective-permute-start | bytes 393224 | tf_op jit(solution)/shard_map/while/body/eval_jaxpr/ppermute | solution.py:15
  482.4 7.4 %collective-permute-start.3 = (f32[128,256]{0,1:T(8,128)S(1)}, f32[128,256]{0,1:T(8,128)S(1)}, u32[]{:S(2)}, u32[]{:S(2)}) collective-permute-start(f32[128,256]{0,1:T(8,128)S(1)} %bitcast_add_fusion.8), channel_id=1, source_target_pairs={{0,28},{4,0},{8,4},{12,8},{16,12},{20,16},{24,20},{28,24},{1,29},{... | collective-permute-start | bytes 393224 | tf_op jit(solution)/shard_map/while/body/eval_jaxpr/ppermute | solution.py:15
  489.7 6.9 %collective-permute-start = (bf16[128,256]{0,1:T(8,128)(2,1)S(1)}, bf16[128,256]{0,1:T(8,128)(2,1)S(1)}, u32[]{:S(2)}, u32[]{:S(2)}) collective-permute-start(bf16[128,256]{0,1:T(8,128)(2,1)S(1)} %copy.122), channel_id=1, source_target_pairs={{0,28},{4,0},{8,4},{12,8},{16,12},{20,16},{24,20},{28,24},{1,29},{... | collective-permute-start | bytes 196616 | tf_op jit(solution)/shard_map/while/body/eval_jaxpr/ppermute | solution.py:15
  493.7 4.9 collective-permute-start.1
  494.7 6.7 %collective-permute-start.2 = (f32[128,256]{0,1:T(8,128)S(1)}, f32[128,256]{0,1:T(8,128)S(1)}, u32[]{:S(2)}, u32[]{:S(2)}) collective-permute-start(f32[128,256]{0,1:T(8,128)S(1)} %bitcast_add_fusion.7), channel_id=1, source_target_pairs={{0,28},{4,0},{8,4},{12,8},{16,12},{20,16},{24,20},{28,24},{1,29},{... | collective-permute-start | bytes 393224 | tf_op jit(solution)/shard_map/while/body/eval_jaxpr/ppermute | solution.py:15
  496.1 7.0 %collective-permute-start.3 = (f32[128,256]{0,1:T(8,128)S(1)}, f32[128,256]{0,1:T(8,128)S(1)}, u32[]{:S(2)}, u32[]{:S(2)}) collective-permute-start(f32[128,256]{0,1:T(8,128)S(1)} %bitcast_add_fusion.8), channel_id=1, source_target_pairs={{0,28},{4,0},{8,4},{12,8},{16,12},{20,16},{24,20},{28,24},{1,29},{... | collective-permute-start | bytes 393224 | tf_op jit(solution)/shard_map/while/body/eval_jaxpr/ppermute | solution.py:15
  503.1 6.6 %collective-permute-start = (bf16[128,256]{0,1:T(8,128)(2,1)S(1)}, bf16[128,256]{0,1:T(8,128)(2,1)S(1)}, u32[]{:S(2)}, u32[]{:S(2)}) collective-permute-start(bf16[128,256]{0,1:T(8,128)(2,1)S(1)} %copy.122), channel_id=1, source_target_pairs={{0,28},{4,0},{8,4},{12,8},{16,12},{20,16},{24,20},{28,24},{1,29},{... | collective-permute-start | bytes 196616 | tf_op jit(solution)/shard_map/while/body/eval_jaxpr/ppermute | solution.py:15
  507.2 5.0 collective-permute-start.1
  508.2 6.5 %collective-permute-start.2 = (f32[128,256]{0,1:T(8,128)S(1)}, f32[128,256]{0,1:T(8,128)S(1)}, u32[]{:S(2)}, u32[]{:S(2)}) collective-permute-start(f32[128,256]{0,1:T(8,128)S(1)} %bitcast_add_fusion.7), channel_id=1, source_target_pairs={{0,28},{4,0},{8,4},{12,8},{16,12},{20,16},{24,20},{28,24},{1,29},{... | collective-permute-start | bytes 393224 | tf_op jit(solution)/shard_map/while/body/eval_jaxpr/ppermute | solution.py:15
  508.5 7.6 %collective-permute-start.3 = (f32[128,256]{0,1:T(8,128)S(1)}, f32[128,256]{0,1:T(8,128)S(1)}, u32[]{:S(2)}, u32[]{:S(2)}) collective-permute-start(f32[128,256]{0,1:T(8,128)S(1)} %bitcast_add_fusion.8), channel_id=1, source_target_pairs={{0,28},{4,0},{8,4},{12,8},{16,12},{20,16},{24,20},{28,24},{1,29},{... | collective-permute-start | bytes 393224 | tf_op jit(solution)/shard_map/while/body/eval_jaxpr/ppermute | solution.py:15
  516.1 6.6 %collective-permute-start = (bf16[128,256]{0,1:T(8,128)(2,1)S(1)}, bf16[128,256]{0,1:T(8,128)(2,1)S(1)}, u32[]{:S(2)}, u32[]{:S(2)}) collective-permute-start(bf16[128,256]{0,1:T(8,128)(2,1)S(1)} %copy.122), channel_id=1, source_target_pairs={{0,28},{4,0},{8,4},{12,8},{16,12},{20,16},{24,20},{28,24},{1,29},{... | collective-permute-start | bytes 196616 | tf_op jit(solution)/shard_map/while/body/eval_jaxpr/ppermute | solution.py:15
  520.1 5.0 collective-permute-start.1
  521.1 5.5 collective-permute-start.2
  521.4 6.7 %collective-permute-start.3 = (f32[128,256]{0,1:T(8,128)S(1)}, f32[128,256]{0,1:T(8,128)S(1)}, u32[]{:S(2)}, u32[]{:S(2)}) collective-permute-start(f32[128,256]{0,1:T(8,128)S(1)} %bitcast_add_fusion.8), channel_id=1, source_target_pairs={{0,28},{4,0},{8,4},{12,8},{16,12},{20,16},{24,20},{28,24},{1,29},{... | collective-permute-start | bytes 393224 | tf_op jit(solution)/shard_map/while/body/eval_jaxpr/ppermute | solution.py:15
  528.0 6.8 %collective-permute-start = (bf16[128,256]{0,1:T(8,128)(2,1)S(1)}, bf16[128,256]{0,1:T(8,128)(2,1)S(1)}, u32[]{:S(2)}, u32[]{:S(2)}) collective-permute-start(bf16[128,256]{0,1:T(8,128)(2,1)S(1)} %copy.122), channel_id=1, source_target_pairs={{0,28},{4,0},{8,4},{12,8},{16,12},{20,16},{24,20},{28,24},{1,29},{... | collective-permute-start | bytes 196616 | tf_op jit(solution)/shard_map/while/body/eval_jaxpr/ppermute | solution.py:15
  532.1 4.6 collective-permute-start.1
  533.1 5.0 collective-permute-start.2
  533.3 6.1 %collective-permute-start.3 = (f32[128,256]{0,1:T(8,128)S(1)}, f32[128,256]{0,1:T(8,128)S(1)}, u32[]{:S(2)}, u32[]{:S(2)}) collective-permute-start(f32[128,256]{0,1:T(8,128)S(1)} %bitcast_add_fusion.8), channel_id=1, source_target_pairs={{0,28},{4,0},{8,4},{12,8},{16,12},{20,16},{24,20},{28,24},{1,29},{... | collective-permute-start | bytes 393224 | tf_op jit(solution)/shard_map/while/body/eval_jaxpr/ppermute | solution.py:15
  539.5 8.0 %collective-permute-start = (bf16[128,256]{0,1:T(8,128)(2,1)S(1)}, bf16[128,256]{0,1:T(8,128)(2,1)S(1)}, u32[]{:S(2)}, u32[]{:S(2)}) collective-permute-start(bf16[128,256]{0,1:T(8,128)(2,1)S(1)} %copy.122), channel_id=1, source_target_pairs={{0,28},{4,0},{8,4},{12,8},{16,12},{20,16},{24,20},{28,24},{1,29},{... | collective-permute-start | bytes 196616 | tf_op jit(solution)/shard_map/while/body/eval_jaxpr/ppermute | solution.py:15
  543.1 4.4 collective-permute-start.1
  544.1 5.3 collective-permute-start.2
  547.0 5.2 collective-permute-start.3
  552.3 7.0 %collective-permute-start = (bf16[128,256]{0,1:T(8,128)(2,1)S(1)}, bf16[128,256]{0,1:T(8,128)(2,1)S(1)}, u32[]{:S(2)}, u32[]{:S(2)}) collective-permute-start(bf16[128,256]{0,1:T(8,128)(2,1)S(1)} %copy.122), channel_id=1, source_target_pairs={{0,28},{4,0},{8,4},{12,8},{16,12},{20,16},{24,20},{28,24},{1,29},{... | collective-permute-start | bytes 196616 | tf_op jit(solution)/shard_map/while/body/eval_jaxpr/ppermute | solution.py:15
  556.5 4.3 collective-permute-start.1
  557.5 5.0 collective-permute-start.2
  557.7 6.1 %collective-permute-start.3 = (f32[128,256]{0,1:T(8,128)S(1)}, f32[128,256]{0,1:T(8,128)S(1)}, u32[]{:S(2)}, u32[]{:S(2)}) collective-permute-start(f32[128,256]{0,1:T(8,128)S(1)} %bitcast_add_fusion.8), channel_id=1, source_target_pairs={{0,28},{4,0},{8,4},{12,8},{16,12},{20,16},{24,20},{28,24},{1,29},{... | collective-permute-start | bytes 393224 | tf_op jit(solution)/shard_map/while/body/eval_jaxpr/ppermute | solution.py:15
  565.0 5.2 collective-permute-start.5
  568.3 4.3 collective-permute-start.4
Sparse Core Ops, SparseCore 0:
  169.7 120.9 all-reduce.2
where the time goes:
time: 582 us; the launch traced here: 581 us
  waiting for transfers between devices  225 us (39%)
  blocking collectives  151 us (26%)
  matrix products  70 us (12%)
  starting transfers between devices  57.7 us (10%)
  local copies, waits for them, and re-layouts  37.8 us (6%)
  other arithmetic  24.8 us (4%)
  between operations  14.4 us (2%)
    all_gather x1, blocking collectives, body(): lax.all_gather(keys, 'ctx', axis=0, tiled=True)  122 us
    psum x1, waiting for transfers between devices, body(): total_grad = lax.psum(dense_part, ('tp', 'ep')) + routed  121 us
    ppermute x30, waiting for transfers between devices, shifted(): lax.ppermute(shard, axis, [(i, (i + by) % devices) for i in range(devices)])  41.8 us
    ppermute x30, starting transfers between devices, shifted(): lax.ppermute(shard, axis, [(i, (i + by) % devices) for i in range(devices)])  40.2 us
    all_to_all x1, waiting for transfers between devices, body(): lax.all_to_all(send_in, 'ctx', split_axis=0, concat_axis=0, tiled=True)  38.5 us
    all_gather x1, blocking collectives, body(): lax.all_gather(values, 'ctx', axis=0, tiled=True)  28.9 us
    all_to_all x1, waiting for transfers between devices, body(): lax.all_to_all(send_grad, 'ctx', split_axis=0, concat_axis=0, tiled=True)  23.2 us
    dot_general x5, matrix products, contract_last(): lax.dot_general(left_rows, right_rows, (((1,), (1,)), ((), ())), preferre...  23.1 us
  transfers between devices with their start and end apart: 34, of which 26 were waited for; matrix products, arithmetic and copies ran while one was open for 9% of the time, Pallas kernels for 0%

commit v1 on v0

v1 whole, which is shorter than its diff:
```python
import functools

import jax
import jax.numpy as jnp
from jax import lax
from jax.experimental import pallas as pl
from jax.experimental.pallas import tpu as pltpu
from jax.sharding import PartitionSpec as P

HEAD_DIM = 128
NEG_FILL = -1e30
EPSILON = 1e-05
MESH = pl.DeviceIdType.MESH
ANY = pl.BlockSpec(memory_space=pl.ANY)
WHOLE = pl.BlockSpec(memory_space=pltpu.VMEM)
BF16 = jnp.bfloat16
F32 = jnp.float32


def contract_last(left_rows, right_rows):
    return lax.dot_general(
        left_rows, right_rows, (((1,), (1,)), ((), ())), preferred_element_type=F32
    )


def round_up(value, step):
    return -(-value // step) * step


def tile_of(hidden, most):
    fits = [t for t in range(16, most + 1, 16) if hidden % t == 0]
    return max(fits) if fits else hidden


class Place:
    def __init__(self, n, tp, ep):
        self.n, self.tp, self.ep = n, tp, ep
        self.c = lax.axis_index("ctx")
        self.t = lax.axis_index("tp")
        self.e = lax.axis_index("ep")

    def ctx_peer(self, k):
        return lax.rem(self.c + k, self.n)

    def ctx_from(self, k):
        return lax.rem(self.c + self.n - k, self.n)

    def ep_peer(self, b):
        return lax.rem(self.e + b, self.ep)

    def ep_from(self, b):
        return lax.rem(self.e + self.ep - b, self.ep)

    def at(self, c=None, t=None, e=None):
        return (
            self.c if c is None else c,
            self.t if t is None else t,
            self.e if e is None else e,
        )

    def greet(self, ctx, group):
        barrier = pltpu.get_barrier_semaphore()
        total = 0
        if ctx:
            for k in range(1, self.n):
                pl.semaphore_signal(
                    barrier, 1, device_id=self.at(c=self.ctx_peer(k)), device_id_type=MESH
                )
            total += self.n - 1
        if group:
            for b in range(1, self.ep):
                pl.semaphore_signal(
                    barrier, 1, device_id=self.at(e=self.ep_peer(b)), device_id_type=MESH
                )
            pl.semaphore_signal(barrier, 1, device_id=self.at(t=1 - self.t), device_id_type=MESH)
            total += self.ep
        pl.semaphore_wait(barrier, total)


def remote(src, dst, send, recv, device):
    return pltpu.make_async_remote_copy(
        src_ref=src, dst_ref=dst, send_sem=send, recv_sem=recv, device_id=device, device_id_type=MESH
    )


def swiglu_tile(x_ref, y_ref, gate_ref, up_ref, down_ref, acc_ref, first):
    a = contract_last(x_ref[...], gate_ref[...])
    b = contract_last(x_ref[...], up_ref[...])
    back = contract_last(y_ref[...], down_ref[...])
    s = jax.nn.sigmoid(a)
    grad_a = (back * b * s * (1.0 + a * (1.0 - s))).astype(BF16)
    grad_b = (back * a * s).astype(BF16)
    width = acc_ref.shape[1]
    step = 512 if width % 512 == 0 else width
    for at in range(0, width, step):
        cols = pl.ds(at, step)
        term = jnp.dot(grad_a, gate_ref[:, cols], preferred_element_type=F32) + jnp.dot(
            grad_b, up_ref[:, cols], preferred_element_type=F32
        )

        @pl.when(first)
        def _():
            acc_ref[:, cols] = term

        @pl.when(jnp.logical_not(first))
        def _():
            acc_ref[:, cols] = acc_ref[:, cols] + term


def dispatch_kernel(
    dims, tiles, rows_ref, x_ref, y_ref, gate_ref, up_ref, down_ref,
    out_ref, part_ref, acc_ref, send1, recv1, send2, recv2, send3, recv3, local
):
    p = Place(*dims)
    step = pl.program_id(0)

    def across(k):
        d = p.ctx_peer(k)
        return remote(rows_ref.at[d], out_ref.at[p.t, p.e, p.c], send1.at[d], recv1.at[p.c], p.at(c=d))

    def arrive(src):
        return remote(
            rows_ref.at[src], out_ref.at[p.t, p.e, src], send1.at[src], recv1.at[src], p.at(c=src)
        )

    def to_ep(b, src, own):
        block = rows_ref.at[src] if own else out_ref.at[p.t, p.e, src]
        return remote(
            block, out_ref.at[p.t, p.e, src], send2.at[b, src], recv2.at[b, src], p.at(e=p.ep_peer(b))
        )

    def from_ep(b, src):
        e = p.ep_from(b)
        return remote(
            out_ref.at[p.t, e, src], out_ref.at[p.t, e, src], send2.at[b, src], recv2.at[b, src], p.at(e=e)
        )

    def to_core(e, src, own=False):
        block = rows_ref.at[src] if own else out_ref.at[p.t, e, src]
        return remote(
            block, out_ref.at[p.t, e, src], send3.at[e, src], recv3.at[e, src], p.at(t=1 - p.t)
        )

    def from_core(e, src):
        block = out_ref.at[1 - p.t, e, src]
        return remote(block, block, send3.at[e, src], recv3.at[e, src], p.at(t=1 - p.t))

    def keep():
        return pltpu.make_async_copy(rows_ref.at[p.c], out_ref.at[p.t, p.e, p.c], local)

    @pl.when(step == 0)
    def _():
        p.greet(True, True)

        @pl.loop(1, p.n)
        def _(k):
            across(k).start()

        for b in range(1, p.ep):
            to_ep(b, p.c, True).start()
        to_core(p.e, p.c, True).start()
        keep().start()

    swiglu_tile(x_ref, y_ref, gate_ref, up_ref, down_ref, acc_ref, step == 0)

    @pl.when(step == tiles - 1)
    def _():
        part_ref[...] = acc_ref[...].astype(BF16)

        def pass_on(src):
            for b in range(1, p.ep):
                from_ep(b, src).wait_recv()
                to_core(p.ep_from(b), src).start()

        @pl.loop(1, p.n)
        def _(k):
            src = p.ctx_from(k)
            arrive(src).wait_recv()
            for b in range(1, p.ep):
                to_ep(b, src, False).start()
            to_core(p.e, src).start()
            pass_on(p.ctx_from(k - 1))

        pass_on(p.ctx_from(p.n - 1))
        keep().wait()

        @pl.loop(0, p.n)
        def _(src):
            for e in range(p.ep):
                from_core(e, src).wait_recv()
                to_core(e, src).wait_send()
            for b in range(1, p.ep):
                to_ep(b, src, False).wait_send()

        @pl.loop(1, p.n)
        def _(k):
            across(k).wait_send()


def expert_kernel(
    dims, tiles, x_ref, y_ref, gate_ref, up_ref, down_ref, kvq_ref,
    out_ref, all_ref, acc_ref, send, recv, local
):
    p = Place(*dims)
    step = pl.program_id(0)

    def across(k):
        d = p.ctx_peer(k)
        return remote(kvq_ref, all_ref.at[p.c], send.at[d], recv.at[p.c], p.at(c=d))

    def arrive(src):
        return remote(kvq_ref, all_ref.at[src], send.at[src], recv.at[src], p.at(c=src))

    def keep():
        return pltpu.make_async_copy(kvq_ref, all_ref.at[p.c], local)

    @pl.when(step == 0)
    def _():
        p.greet(True, False)

        @pl.loop(1, p.n)
        def _(k):
            across(k).start()

        keep().start()

    swiglu_tile(x_ref, y_ref, gate_ref.at[0], up_ref.at[0], down_ref.at[0], acc_ref, step == 0)

    @pl.when(step == tiles - 1)
    def _():
        out_ref[...] = acc_ref[...].astype(BF16)
        keep().wait()

        @pl.loop(1, p.n)
        def _(k):
            arrive(p.ctx_from(k)).wait_recv()
            across(k).wait_send()


def return_kernel(
    dims, chunks, part_ref, back_ref, dense_ref,
    core_buf, ep_out, ep_in, fin_ref, send1, recv1, send2, recv2, send3, recv3
):
    p = Place(*dims)
    p.greet(True, True)

    def to_core(e, i):
        return remote(
            part_ref.at[1 - p.t, e, i], core_buf.at[e, i], send1.at[e, i], recv1.at[e, i], p.at(t=1 - p.t)
        )

    def to_ep(b, i):
        return remote(
            ep_out.at[b, i], ep_in.at[b, i], send2.at[b, i], recv2.at[b, i], p.at(e=p.ep_peer(b))
        )

    def home(d):
        return remote(fin_ref.at[d], back_ref.at[p.c], send3.at[d], recv3.at[p.c], p.at(c=d))

    def arrive(src):
        return remote(fin_ref.at[src], back_ref.at[src], send3.at[src], recv3.at[src], p.at(c=src))

    def chunk_of(k):
        return jnp.where(k < p.n, lax.rem(p.c + k + 1, p.n), k)

    @pl.loop(0, chunks)
    def _(k):
        i = chunk_of(k)
        for b in range(1, p.ep):
            to_core(p.ep_peer(b), i).start()
        to_core(p.e, i).start()

    @pl.loop(0, chunks)
    def _(k):
        i = chunk_of(k)
        for b in range(1, p.ep):
            e = p.ep_peer(b)
            to_core(e, i).wait_recv()
            ep_out[b, i] = (part_ref[p.t, e, i].astype(F32) + core_buf[e, i].astype(F32)).astype(BF16)
            to_ep(b, i).start()

    def total(i):
        to_core(p.e, i).wait_recv()
        value = part_ref[p.t, p.e, i].astype(F32) + core_buf[p.e, i].astype(F32)
        for b in range(1, p.ep):
            to_ep(b, i).wait_recv()
            value = value + ep_in[b, i].astype(F32)
        return value

    @pl.loop(0, p.n - 1)
    def _(k):
        i = chunk_of(k)
        fin_ref[i] = total(i).astype(BF16)
        home(i).start()

    back_ref[p.c] = total(p.c).astype(BF16)

    @pl.loop(p.n, chunks)
    def _(i):
        dense_ref[i - p.n] = total(i)

    @pl.loop(1, p.n)
    def _(k):
        arrive(p.ctx_from(k)).wait_recv()
        home(p.ctx_peer(k)).wait_send()

    @pl.loop(0, chunks)
    def _(i):
        for b in range(1, p.ep):
            to_ep(b, i).wait_send()
        for e in range(p.ep):
            to_core(e, i).wait_send()


def group_kernel(dims, own_ref, all_ref, send2, recv2, send3, recv3):
    p = Place(*dims)
    p.greet(False, True)
    all_ref[p.t, p.e] = own_ref[...]

    def to_ep(b):
        return remote(own_ref, all_ref.at[p.t, p.e], send2.at[b], recv2.at[b], p.at(e=p.ep_peer(b)))

    def from_ep(b):
        e = p.ep_from(b)
        return remote(own_ref, all_ref.at[p.t, e], send2.at[b], recv2.at[b], p.at(e=e))

    def to_core(e, own=False):
        block = own_ref if own else all_ref.at[p.t, e]
        return remote(block, all_ref.at[p.t, e], send3.at[e], recv3.at[e], p.at(t=1 - p.t))

    def from_core(e):
        block = all_ref.at[1 - p.t, e]
        return remote(block, block, send3.at[e], recv3.at[e], p.at(t=1 - p.t))

    for b in range(1, p.ep):
        to_ep(b).start()
    to_core(p.e, True).start()
    for b in range(1, p.ep):
        from_ep(b).wait_recv()
        to_core(p.ep_from(b)).start()
    for e in range(p.ep):
        from_core(e).wait_recv()
        to_core(e).wait_send()
    for b in range(1, p.ep):
        to_ep(b).wait_send()


def attention_kernel(
    dims, g_ref, kvq_ref, dq_ref, dk_ref, dv_ref, g_all, stats, mine, send1, recv1, send2, recv2
):
    p = Place(*dims)
    p.greet(True, False)
    n = p.n
    rows, width = g_ref.shape
    heads = width // HEAD_DIM
    seq = n * rows
    scale = HEAD_DIM ** (-0.5)

    def across(k):
        d = p.ctx_peer(k)
        return remote(g_ref, g_all.at[p.c], send1.at[d], recv1.at[p.c], p.at(c=d))

    def across_stats(k):
        d = p.ctx_peer(k)
        return remote(mine, stats.at[p.c], send2.at[d], recv2.at[p.c], p.at(c=d))

    def arrive(src):
        return remote(g_ref, g_all.at[src], send1.at[src], recv1.at[src], p.at(c=src))

    def arrive_stats(src):
        return remote(mine, stats.at[src], send2.at[src], recv2.at[src], p.at(c=src))

    @pl.loop(1, n)
    def _(k):
        across(k).start()

    g_all[p.c] = g_ref[...]
    mine[...] = jnp.zeros_like(mine)
    query_at = p.c * rows + lax.broadcasted_iota(jnp.int32, (rows, seq), 0)
    key_at = lax.broadcasted_iota(jnp.int32, (rows, seq), 1)
    allowed = key_at <= query_at
    for h in range(heads):
        cols = pl.ds(h * HEAD_DIM, HEAD_DIM)
        keys = kvq_ref[:, :, h * HEAD_DIM:(h + 1) * HEAD_DIM].reshape(seq, HEAD_DIM)
        values = kvq_ref[:, :, width + h * HEAD_DIM:width + (h + 1) * HEAD_DIM].reshape(seq, HEAD_DIM)
        q = kvq_ref[p.c, :, pl.ds(2 * width + h * HEAD_DIM, HEAD_DIM)]
        scores = jnp.where(allowed, contract_last(q, keys) * scale, NEG_FILL)
        top = jnp.max(scores, axis=1, keepdims=True)
        weights = jnp.where(allowed, jnp.exp(scores - top), 0.0)
        total = jnp.sum(weights, axis=1, keepdims=True)
        probs = weights / total
        grad_probs = contract_last(g_ref[:, cols], values)
        delta = jnp.sum(probs * grad_probs, axis=1, keepdims=True)
        log_norm = top + jnp.log(total)
        mine[h:h + 1, :] = jnp.transpose(jnp.broadcast_to(delta, (rows, 128)))[0:1, :]
        mine[heads + h:heads + h + 1, :] = jnp.transpose(jnp.broadcast_to(log_norm, (rows, 128)))[0:1, :]
        grad_scores = (probs * (grad_probs - delta)).astype(BF16)
        dq_ref[:, cols] = (jnp.dot(grad_scores, keys, preferred_element_type=F32) * scale).astype(BF16)

    @pl.loop(1, n)
    def _(k):
        across_stats(k).start()

    stats[p.c] = mine[...]

    @pl.loop(1, n)
    def _(k):
        arrive(p.ctx_from(k)).wait_recv()
        arrive_stats(p.ctx_from(k)).wait_recv()

    key_at = p.c * rows + lax.broadcasted_iota(jnp.int32, (rows, seq), 0)
    query_at = lax.broadcasted_iota(jnp.int32, (rows, seq), 1)
    allowed = key_at <= query_at
    for h in range(heads):
        cols = pl.ds(h * HEAD_DIM, HEAD_DIM)
        queries = kvq_ref[:, :, 2 * width + h * HEAD_DIM:2 * width + (h + 1) * HEAD_DIM].reshape(
            seq, HEAD_DIM
        )
        upstream = g_all[:, :, h * HEAD_DIM:(h + 1) * HEAD_DIM].reshape(seq, HEAD_DIM)
        keys = kvq_ref[p.c, :, pl.ds(h * HEAD_DIM, HEAD_DIM)]
        values = kvq_ref[p.c, :, pl.ds(width + h * HEAD_DIM, HEAD_DIM)]
        delta = jnp.concatenate([stats[s, h:h + 1, :] for s in range(n)], axis=1)
        log_norm = jnp.concatenate([stats[s, heads + h:heads + h + 1, :] for s in range(n)], axis=1)
        scores = contract_last(keys, queries) * scale
        probs = jnp.where(allowed, jnp.exp(jnp.where(allowed, scores - log_norm, 0.0)), 0.0)
        grad_scores = (probs * (contract_last(values, upstream) - delta)).astype(BF16)
        dv_ref[:, cols] = jnp.dot(probs.astype(BF16), upstream, preferred_element_type=F32).astype(BF16)
        dk_ref[:, cols] = (jnp.dot(grad_scores, queries, preferred_element_type=F32) * scale).astype(BF16)

    @pl.loop(1, n)
    def _(k):
        across(k).wait_send()
        across_stats(k).wait_send()


def params(collective_id, grid=False):
    return pltpu.CompilerParams(
        collective_id=collective_id,
        has_side_effects=True,
        vmem_limit_bytes=56 * 1024 * 1024,
        **({"dimension_semantics": ("arbitrary",)} if grid else {}),
    )


def body(
    dims, hidden, grad_out, gain, dense_gate, dense_up, dense_down, expert_gate, expert_up, expert_down,
    out_proj, queries, keys, values, route_ids, route_weights
):
    n, tp, ep = dims
    group = tp * ep
    rows, width = hidden.shape
    part = width // group
    picks = route_ids.shape[1]
    capacity = 5 * rows // (2 * n)
    pair = round_up(2 * capacity, 16)
    chunk = round_up(capacity, 16)
    sem = pltpu.SemaphoreType.DMA
    at = lax.axis_index("tp") * ep + lax.axis_index("ep")

    hidden_f = hidden.astype(F32)
    inverse = lax.rsqrt(jnp.mean(hidden_f * hidden_f, axis=1, keepdims=True) + EPSILON)
    normed = hidden_f * inverse
    mixed_in = (normed * gain).astype(BF16)

    flat_ids = route_ids.reshape(-1)
    hits = (flat_ids[:, None] == lax.iota(jnp.int32, n)[None, :]).astype(BF16)
    order = lax.iota(jnp.int32, picks * rows)
    before = (order[None, :] < order[:, None]).astype(BF16)
    earlier = jnp.dot(before, hits, preferred_element_type=F32)
    slots = jnp.sum(earlier * hits.astype(F32), axis=1).astype(jnp.int32)
    slots = slots.reshape(rows, picks)
    pair_at = (route_ids * pair + slots).T
    home_at = route_ids * chunk + slots
    places = lax.iota(jnp.int32, n * pair)[:, None]
    own_in = lax.dynamic_slice(mixed_in, (0, at * part), (rows, part))
    own_out = lax.dynamic_slice(grad_out, (0, at * part), (rows, part))
    pick_in = sum((places == pair_at[k][None, :]).astype(BF16) for k in range(picks))
    pick_out = [(places == pair_at[k][None, :] + capacity) for k in range(picks)]
    weight_of = sum(
        jnp.sum(jnp.where(pick_out[k], route_weights[:, k][None, :], 0.0), axis=1, keepdims=True)
        for k in range(picks)
    )
    pick_out = sum(hit.astype(BF16) for hit in pick_out)
    send_rows = (
        jnp.dot(pick_in, own_in, preferred_element_type=F32)
        + jnp.dot(pick_out, own_out, preferred_element_type=F32) * weight_of
    ).astype(BF16).reshape(n, pair, part)

    ff = dense_gate.shape[0]
    ff_tile = tile_of(ff, 320)
    weight_spec = pl.BlockSpec((ff_tile, width), lambda i: (i, 0))
    full = pl.BlockSpec((rows, width), lambda i: (0, 0))
    arrived, dense_part = pl.pallas_call(
        functools.partial(dispatch_kernel, dims, ff // ff_tile),
        grid=(ff // ff_tile,),
        out_shape=(
            jax.ShapeDtypeStruct((tp, ep, n, pair, part), BF16),
            jax.ShapeDtypeStruct((rows, width), BF16),
        ),
        in_specs=[ANY, full, full, weight_spec, weight_spec, weight_spec],
        out_specs=(ANY, full),
        scratch_shapes=[pltpu.VMEM((rows, width), F32)]
        + [sem((n,))] * 2 + [sem((ep, n))] * 4 + [sem],
        compiler_params=params(1, True),
        name="dispatch_dense",
    )(send_rows, mixed_in, grad_out, dense_gate, dense_up, dense_down)

    arrived = arrived.reshape(group, n, pair, part)

    def joined(low):
        return arrived[:, :, low:low + capacity].transpose(1, 2, 0, 3).reshape(n * capacity, width)

    kvq = jnp.concatenate([keys, values, queries], axis=1)
    head_width = queries.shape[1]
    eh = expert_gate.shape[1]
    eh_tile = tile_of(eh, 320)
    weight_spec = pl.BlockSpec((1, eh_tile, width), lambda i: (0, i, 0))
    full = pl.BlockSpec((n * capacity, width), lambda i: (0, 0))
    expert_part, kvq_all = pl.pallas_call(
        functools.partial(expert_kernel, dims, eh // eh_tile),
        grid=(eh // eh_tile,),
        out_shape=(
            jax.ShapeDtypeStruct((n * capacity, width), BF16),
            jax.ShapeDtypeStruct((n, rows, 3 * head_width), BF16),
        ),
        in_specs=[full, full, weight_spec, weight_spec, weight_spec, ANY],
        out_specs=(full, ANY),
        scratch_shapes=[pltpu.VMEM((n * capacity, width), F32)] + [sem((n,))] * 2 + [sem],
        compiler_params=params(2, True),
        name="expert_gather",
    )(joined(0), joined(capacity), expert_gate, expert_up, expert_down, kvq)

    dense_chunks = -(-rows // chunk)
    chunks = n + dense_chunks
    expert_part = jnp.pad(
        expert_part.reshape(n, capacity, group, part), ((0, 0), (0, chunk - capacity), (0, 0), (0, 0))
    )
    dense_part = jnp.pad(
        dense_part.reshape(rows, group, part), ((0, dense_chunks * chunk - rows), (0, 0), (0, 0))
    ).reshape(dense_chunks, chunk, group, part)
    parts = jnp.concatenate([expert_part, dense_part], axis=0).transpose(2, 0, 1, 3)
    parts = parts.reshape(tp, ep, chunks, chunk, part)
    returned, dense_sum = pl.pallas_call(
        functools.partial(return_kernel, dims, chunks),
        out_shape=(
            jax.ShapeDtypeStruct((n, chunk, part), BF16),
            jax.ShapeDtypeStruct((dense_chunks, chunk, part), F32),
        ),
        in_specs=[WHOLE],
        out_specs=(WHOLE, WHOLE),
        scratch_shapes=[
            pltpu.VMEM((ep, chunks, chunk, part), BF16),
            pltpu.VMEM((ep, chunks, chunk, part), BF16),
            pltpu.VMEM((ep, chunks, chunk, part), BF16),
            pltpu.VMEM((n, chunk, part), BF16),
        ]
        + [sem((ep, chunks))] * 4 + [sem((n,))] * 2,
        compiler_params=params(3),
        name="return_rows",
    )(parts)

    home_places = lax.iota(jnp.int32, n * chunk)[None, :]
    take = sum((home_places == home_at[:, k:k + 1]).astype(BF16) for k in range(picks))
    own_total = (
        jnp.dot(take, returned.reshape(n * chunk, part), preferred_element_type=F32)
        + dense_sum.reshape(dense_chunks * chunk, part)[:rows]
    ).astype(BF16)
    total_grad = pl.pallas_call(
        functools.partial(group_kernel, dims),
        out_shape=jax.ShapeDtypeStruct((tp, ep, rows, part), BF16),
        in_specs=[WHOLE],
        out_specs=WHOLE,
        scratch_shapes=[sem((ep,))] * 4,
        compiler_params=params(4),
        name="group_gather",
    )(own_total)
    total_grad = total_grad.reshape(group, rows, part).transpose(1, 0, 2).reshape(rows, width).astype(F32)
    scaled_grad = total_grad * gain
    grad_hidden = (
        grad_out.astype(F32)
        + inverse * (scaled_grad - normed * jnp.mean(scaled_grad * normed, axis=1, keepdims=True))
    ).astype(BF16)
    grad_heads = contract_last(grad_hidden, out_proj).astype(BF16)

    heads = head_width // HEAD_DIM
    stat_rows = round_up(2 * heads, 8)
    grads = jax.ShapeDtypeStruct((rows, head_width), BF16)
    grad_queries, grad_keys, grad_values = pl.pallas_call(
        functools.partial(attention_kernel, dims),
        out_shape=(grads, grads, grads),
        in_specs=[WHOLE, WHOLE],
        out_specs=(WHOLE, WHOLE, WHOLE),
        scratch_shapes=[
            pltpu.VMEM((n, rows, head_width), BF16),
            pltpu.VMEM((n, stat_rows, rows), F32),
            pltpu.VMEM((stat_rows, rows), F32),
        ]
        + [sem((n,))] * 4,
        compiler_params=params(5),
        name="attention_grads",
    )(grad_heads, kvq_all)
    return (grad_hidden, grad_queries, grad_keys, grad_values)


def solution(mesh):
    dims = (mesh.shape["ctx"], mesh.shape["tp"], mesh.shape["ep"])
    hidden_units = P(("tp", "ep"), None)
    expert_units = P("ctx", ("tp", "ep"), None)
    by_head = P("ctx", ("tp", "ep"))
    return jax.shard_map(
        functools.partial(body, dims),
        mesh=mesh,
        in_specs=(
            P("ctx", None), P("ctx", None), P(),
            hidden_units, hidden_units, hidden_units,
            expert_units, expert_units, expert_units,
            hidden_units, by_head, by_head, by_head,
            P("ctx", None), P("ctx", None),
        ),
        out_specs=(P("ctx", None), by_head, by_head, by_head),
        check_vma=False,
    )
```

time: 582 us -> 202 us (0.35)
  waiting for transfers between devices: 225 us -> 0 us
  Pallas kernels: 0 us -> 161 us
  blocking collectives: 151 us -> 0 us
  matrix products: 70 us -> 6.75 us
  starting transfers between devices: 57.7 us -> 0 us
  other arithmetic: 24.8 us -> 8.95 us
  local copies, waits for them, and re-layouts: 37.8 us -> 23.6 us
  between operations: 14.4 us -> 0.88 us
    pallas_call x0 -> x5, Pallas kernels: none -> 161 us  [the longest x1 48.5 us: body(): pl.pallas_call(functools.partial(dispatch_kernel, dims, ff // ff_tile), g...]
    all_gather x2 -> x0, blocking collectives: 151 us -> none  [the longest x1 122 us: body(): lax.all_gather(keys, 'ctx', axis=0, tiled=True)]
    psum x1 -> x0, waiting for transfers between devices: 121 us -> none  [body(): total_grad = lax.psum(dense_part, ('tp', 'ep')) + routed]
    all_to_all x3 -> x0, waiting for transfers between devices: 61.6 us -> none  [the longest x1 38.5 us: body(): lax.all_to_all(send_in, 'ctx', split_axis=0, concat_axis=0, tiled=True)]
    ppermute x30 -> x0, waiting for transfers between devices: 41.8 us -> none  [shifted(): lax.ppermute(shard, axis, [(i, (i + by) % devices) for i in range(devices)])]
    dot_general x46 -> x4, matrix products: 46.9 us -> 5.41 us  [the longest x1 2.49 us: body(): jnp.dot(pick_out, own_out, preferred_element_type=F32) * weight_of]
    ppermute x30 -> x0, starting transfers between devices: 40.2 us -> none  [shifted(): lax.ppermute(shard, axis, [(i, (i + by) % devices) for i in range(devices)])]
    dot_general x5 -> x1, matrix products: 23.1 us -> 1.34 us  [contract_last(): lax.dot_general(left_rows, right_rows, (((1,), (1,)), ((), ())), preferre...]
  transfers between devices with their start and end apart: 34 -> 0, of which waited for: 26 -> 0; matrix products, arithmetic and copies ran while one was open for 9% -> 0% of each run, Pallas kernels for 0% -> 0%
where the time goes in v1:
time: 202 us; the launch traced here: 201 us
  Pallas kernels  161 us (80%)
  local copies, waits for them, and re-layouts  23.6 us (12%)
  other arithmetic  8.95 us (4%)
  matrix products  6.75 us (3%)
    pallas_call x1, Pallas kernels, body(): pl.pallas_call(functools.partial(dispatch_kernel, dims, ff // ff_tile), g...  48.5 us
    pallas_call x1, Pallas kernels, body(): pl.pallas_call(functools.partial(expert_kernel, dims, eh // eh_tile), gri...  41.6 us
    pallas_call x1, Pallas kernels, body(): pl.pallas_call(functools.partial(return_kernel, dims, chunks), out_shape=...  39.6 us
    pallas_call x1, Pallas kernels, body(): pl.pallas_call(functools.partial(attention_kernel, dims), out_shape=(grad...  20.1 us
    unnamed x28, local copies, waits for them, and re-layouts  13.3 us
    pallas_call x1, Pallas kernels, body(): pl.pallas_call(functools.partial(group_kernel, dims), out_shape=jax.Shape...  10.9 us
    reshape x2, local copies, waits for them, and re-layouts, body(): expert_part.reshape(n, capacity, group, part)  6.05 us

profile of v1, /device:TPU:0, one launch (start us, length us, event | category | flops | bytes accessed | tf_op | source)
XLA Modules:
  0.0 200.9 jit_solution(17131459228515946213)
XLA Ops:
  0.6 0.0 copy-start
  0.6 0.9 copy.54
  1.6 0.1 eq.106
  1.7 0.2 fusion.13
  1.9 0.1 convert_element_type.74
  2.1 0.1 copy.55
  2.1 0.7 multiply_add_fusion
  2.8 0.8 slice_bitcast_fusion
  3.6 0.2 select_reduce_fusion
  3.9 1.4 fusion.11
  5.3 1.5 fusion.5.x_ref
  6.8 0.0 copy-start.3
  6.8 0.5 fusion.19
  7.3 2.5 %add_convert_fusion = bf16[640,896]{1,0:T(8,128)(2,1)} fusion(f32[640,896]{1,0:T(8,128)S(1)} %fusion.19, f32[640]{0:T(1024)S(1)} %add.71, bf16[128,3584]{1,0:T(8,128)(2,1)} %y_ref.1, s32[]{:T(128)S(6)} %select_n.11, s32[128]{0:T(128)S(1)} %get-tuple-element.28, s32[128]{0:T(128)S(1)} %get-tuple-element.29), kind=kOutput, calls=%fused_computation.3 | convolution fusion | flops 149176320 | bytes 3673604 | tf_op jit(solution)/shard_map/dot_general | solution.py:486
  9.8 48.5 %dispatch_dense.1 = (bf16[2,2,8,80,896]{4,3,2,1,0:T(8,128)(2,1)}, bf16[128,3584]{1,0:T(8,128)(2,1)}) custom-call(bf16[8,80,896]{2,1,0:T(8,128)(2,1)} %bitcast.56, bf16[128,3584]{1,0:T(8,128)(2,1)} %copy-done.3, bf16[128,3584]{1,0:T(8,128)(2,1)} %y_ref.1, bf16[608,3584]{1,0:T(8,128)(2,1)} %gate_ref.2, bf16[608,3584]{1,0:T(8,128)(2,1)} %up_ref.2, ...), custom_call_target="tpu_custom_call" | custom-call | tf_op jit(solution)/shard_map/dispatch_dense/pallas_call | solution.py:493
  58.3 2.7 %fusion.42 = (bf16[4,8,40,896]{3,2,1,0:T(8,128)(2,1)S(1)}, bf16[4,8,40,896]{3,2,1,0:T(8,128)(2,1)S(1)}) fusion(bf16[4,8,80,896]{3,2,1,0:T(8,128)(2,1)} %bitcast.55), kind=kLoop, calls=%fused_computation.68 | loop fusion | bytes 9175040 | tf_op jit(solution)/shard_map/slice | solution.py:511
  61.0 1.8 copy.62
  62.8 1.7 copy.67
  64.5 1.8 copy.63
  66.3 0.0 copy-start.7
  66.3 0.0 copy-start.8
  66.3 0.0 copy-start.9
  66.3 1.8 copy.68
  68.1 0.7 pad_maximum_fusion.kvq_ref
  68.8 41.6 %expert_gather.1 = (bf16[320,3584]{1,0:T(8,128)(2,1)}, bf16[8,128,768]{2,1,0:T(8,128)(2,1)}) custom-call(bf16[320,3584]{1,0:T(8,128)(2,1)} %bitcast.51, bf16[320,3584]{1,0:T(8,128)(2,1)} %bitcast.52, bf16[1,960,3584]{2,1,0:T(8,128)(2,1)} %gate_ref.3, bf16[1,960,3584]{2,1,0:T(8,128)(2,1)} %up_ref.3, bf16[1,960,3584]{2,1,0:T(8,128)(2,1)} %down_ref.3, ...), custom_call_target="tpu_custom_call" | custom-call | tf_op jit(solution)/shard_map/expert_gather/pallas_call | solution.py:519
  110.4 4.0 %reshape.73 = bf16[8,40,4,896]{3,2,1,0:T(4,128)(2,1)} reshape(bf16[320,3584]{1,0:T(8,128)(2,1)} %get-tuple-element.14) | data formatting | bytes 4587520 | tf_op jit(solution)/shard_map/reshape | solution.py:536
  114.4 2.0 copy.59
  116.4 0.0 copy-done.5
  116.4 0.1 copy.70
  116.5 0.1 pad.9.clone
  116.6 2.0 fusion.1
  118.6 39.6 %return_rows.1 = (bf16[8,48,896]{2,1,0:T(8,128)(2,1)}, f32[3,48,896]{2,1,0:T(8,128)}) custom-call(bf16[2,2,11,48,896]{4,3,2,1,0:T(8,128)(2,1)} %bitcast.50), custom_call_target="tpu_custom_call" | custom-call | tf_op jit(solution)/shard_map/return_rows/pallas_call | solution.py:543
  158.2 2.3 %fusion.12.own_ref = bf16[128,896]{1,0:T(8,128)(2,1)} fusion(bf16[384,896]{1,0:T(8,128)(2,1)} %bitcast.60, f32[144,896]{1,0:T(8,128)} %bitcast.61, s32[128]{0:T(128)S(1)} %get-tuple-element.27, s32[128]{0:T(128)S(1)} %get-tuple-element.26), kind=kOutput, calls=%fused_computation.18 | convolution fusion | flops 88702976 | bytes 1377280 | tf_op jit(solution)/shard_map/dot_general | solution.py:565
  160.5 10.9 %group_gather.1 = bf16[2,2,128,896]{3,2,1,0:T(8,128)(2,1)} custom-call(bf16[128,896]{1,0:T(8,128)(2,1)} %fusion.12.own_ref), custom_call_target="tpu_custom_call" | custom-call | tf_op jit(solution)/shard_map/group_gather/pallas_call | solution.py:568
  171.4 1.3 convert_bitcast_fusion
  172.7 0.0 copy-start.1
  172.7 0.0 copy-start.6
  172.8 0.2 copy.66
  173.0 0.0 copy-start.2
  173.0 0.9 copy-done.1
  173.9 0.4 fusion.6
  174.4 0.6 fusion.10
  175.0 0.0 copy-start.4
  175.0 1.3 convolution_convert_fusion.g_ref
  176.4 20.1 %attention_grads.1 = (bf16[128,256]{1,0:T(8,128)(2,1)}, bf16[128,256]{1,0:T(8,128)(2,1)}, bf16[128,256]{1,0:T(8,128)(2,1)}) custom-call(bf16[128,256]{1,0:T(8,128)(2,1)} %convolution_convert_fusion.g_ref, bf16[8,128,768]{2,1,0:T(8,128)(2,1)} %get-tuple-element.18.kvq_ref), custom_call_target="tpu_custom_call" | custom-call | tf_op jit(solution)/shard_map/attention_grads/pallas_call | solution.py:588
  196.5 1.5 copy.74
  198.0 1.5 copy.75
  199.4 1.5 copy.76
  (15 shorter events, 0.1 us)
Async XLA Ops:
  0.6 174.4 %copy-start = (bf16[256,3584]{1,0:T(8,128)(2,1)S(1)}, bf16[256,3584]{1,0:T(8,128)(2,1)}, u32[]{:S(2)}) copy-start(bf16[256,3584]{1,0:T(8,128)(2,1)} %param.24) | copy-start | bytes 5505028
  6.8 3.0 %copy-start.3 = (bf16[128,3584]{1,0:T(8,128)(2,1)}, bf16[128,3584]{1,0:T(8,128)(2,1)S(1)}, u32[]{:S(2)}) copy-start(bf16[128,3584]{1,0:T(8,128)(2,1)S(1)} %fusion.5.x_ref) | copy-start | bytes 2752516
  66.3 1.8 copy-start.7
  66.3 1.8 copy-start.8
  66.3 1.8 copy-start.9
  114.4 2.0 %copy-start.5 = (bf16[128,3584]{1,0:T(8,128)(2,1)S(1)}, bf16[128,3584]{1,0:T(8,128)(2,1)}, u32[]{:S(2)}) copy-start(bf16[128,3584]{1,0:T(8,128)(2,1)} %get-tuple-element.15) | copy-start | bytes 2752516
  172.7 1.2 copy-start.1
  172.7 1.2 copy-start.6
  173.0 1.4 copy-start.2
  175.0 23.0 %copy-start.4 = (bf16[128,3584]{1,0:T(8,128)(2,1)}, bf16[128,3584]{1,0:T(8,128)(2,1)S(1)}, u32[]{:S(2)}) copy-start(bf16[128,3584]{1,0:T(8,128)(2,1)S(1)} %fusion.10) | copy-start | bytes 2752516

commit v2 on v1

--- a/solution.py
+++ b/solution.py
@@ -312,6 +312,297 @@
             to_core(e, i).wait_send()
 
 
+def experts_kernel(
+    dims, capacity, rows_ref, x_ref, y_ref, dense_gate, dense_up, dense_down,
+    expert_gate, expert_up, expert_down, kvq_ref, back_ref, dense_ref, all_ref,
+    got, x_in, y_in, weights, grad_a, grad_b, out, core_buf, ep_out, ep_in, fin_ref,
+    send1, recv1, send2, recv2, send3, recv3, send4, recv4, send5, recv5, send6, recv6,
+    send7, recv7, send8, recv8, loads, local
+):
+    p = Place(*dims)
+    n = p.n
+    part = rows_ref.shape[2]
+    rows, width = x_ref.shape
+    ff, eh = dense_gate.shape[0], expert_gate.shape[1]
+    chunks, chunk = out.shape[0], out.shape[1]
+    head_width = kvq_ref.shape[1] // 3
+
+    def cols(t, e):
+        return pl.ds(pl.multiple_of((t * p.ep + e) * part, 128), part)
+
+    def across(k):
+        d = p.ctx_peer(k)
+        return remote(
+            rows_ref.at[d], got.at[p.c, :, cols(p.t, p.e)], send1.at[d], recv1.at[p.c], p.at(c=d)
+        )
+
+    def arrive(src):
+        return remote(
+            rows_ref.at[src], got.at[src, :, cols(p.t, p.e)], send1.at[src], recv1.at[src], p.at(c=src)
+        )
+
+    def to_ep(b, src, own=False):
+        slot = got.at[src, :, cols(p.t, p.e)]
+        return remote(
+            rows_ref.at[src] if own else slot, slot, send2.at[b, src], recv2.at[b, src],
+            p.at(e=p.ep_peer(b)),
+        )
+
+    def from_ep(b, src):
+        e = p.ep_from(b)
+        slot = got.at[src, :, cols(p.t, e)]
+        return remote(slot, slot, send2.at[b, src], recv2.at[b, src], p.at(e=e))
+
+    def to_core(e, src, own=False):
+        slot = got.at[src, :, cols(p.t, e)]
+        return remote(
+            rows_ref.at[src] if own else slot, slot, send3.at[e, src], recv3.at[e, src], p.at(t=1 - p.t)
+        )
+
+    def from_core(e, src):
+        slot = got.at[src, :, cols(1 - p.t, e)]
+        return remote(slot, slot, send3.at[e, src], recv3.at[e, src], p.at(t=1 - p.t))
+
+    def keep():
+        return pltpu.make_async_copy(rows_ref.at[p.c], got.at[p.c, :, cols(p.t, p.e)], local.at[0])
+
+    def pass_on(src):
+        for b in range(1, p.ep):
+            from_ep(b, src).wait_recv()
+            to_core(p.ep_from(b), src).start()
+
+    def forward(k):
+        src = p.ctx_from(k)
+        arrive(src).wait_recv()
+        for b in range(1, p.ep):
+            to_ep(b, src).start()
+        to_core(p.e, src).start()
+        pass_on(p.ctx_from(k - 1))
+
+    def sum_core(e, i):
+        return remote(
+            out.at[i, :, cols(1 - p.t, e)], core_buf.at[e, i], send4.at[e, i], recv4.at[e, i],
+            p.at(t=1 - p.t),
+        )
+
+    def sum_ep(b, i):
+        return remote(
+            ep_out.at[b - 1, i], ep_in.at[b - 1, i], send5.at[b, i], recv5.at[b, i], p.at(e=p.ep_peer(b))
+        )
+
+    def pass_sum(b, i):
+        e = p.ep_peer(b)
+        sum_core(e, i).wait_recv()
+        ep_out[b - 1, i] = (out[i, :, cols(p.t, e)].astype(F32) + core_buf[e, i].astype(F32)).astype(BF16)
+        sum_ep(b, i).start()
+
+    def total(i):
+        sum_core(p.e, i).wait_recv()
+        value = out[i, :, cols(p.t, p.e)].astype(F32) + core_buf[p.e, i].astype(F32)
+        for b in range(1, p.ep):
+            sum_ep(b, i).wait_recv()
+            value = value + ep_in[b - 1, i].astype(F32)
+        return value
+
+    def home(d):
+        return remote(fin_ref.at[d], back_ref.at[p.c], send6.at[d], recv6.at[p.c], p.at(c=d))
+
+    def home_from(src):
+        return remote(fin_ref.at[src], back_ref.at[src], send6.at[src], recv6.at[src], p.at(c=src))
+
+    def keys_to(d):
+        at = pl.ds(0, 2 * head_width)
+        return remote(
+            kvq_ref.at[:, at], all_ref.at[p.c, :, at], send7.at[d], recv7.at[p.c], p.at(c=d)
+        )
+
+    def keys_from(src):
+        at = pl.ds(0, 2 * head_width)
+        return remote(
+            kvq_ref.at[:, at], all_ref.at[src, :, at], send7.at[src], recv7.at[src], p.at(c=src)
+        )
+
+    def queries_to(d):
+        at = pl.ds(2 * head_width, head_width)
+        return remote(
+            kvq_ref.at[:, at], all_ref.at[p.c, :, at], send8.at[d], recv8.at[p.c], p.at(c=d)
+        )
+
+    def queries_from(src):
+        at = pl.ds(2 * head_width, head_width)
+        return remote(
+            kvq_ref.at[:, at], all_ref.at[src, :, at], send8.at[src], recv8.at[src], p.at(c=src)
+        )
+
+    def keep_kvq():
+        return pltpu.make_async_copy(kvq_ref, all_ref.at[p.c], local.at[1])
+
+    def load(j, ref, size):
+        return pltpu.make_async_copy(ref, weights.at[j, pl.ds(0, size)], loads.at[j])
+
+    dense = [load(j, ref, ff) for j, ref in enumerate((dense_gate, dense_up, dense_down))]
+    expert = [
+        load(j, ref.at[0], eh) for j, ref in enumerate((expert_gate, expert_up, expert_down))
+    ]
+    for copy in dense:
+        copy.start()
+    p.greet(True, True)
+
+    @pl.loop(1, n)
+    def _(k):
+        across(k).start()
+
+    for b in range(1, p.ep):
+        to_ep(b, p.c, True).start()
+    to_core(p.e, p.c, True).start()
+    keep().start()
+    keep_kvq().start()
+
+    def slopes(a, b, back):
+        s = jax.nn.sigmoid(a)
+        return (back * b * s * (1.0 + a * (1.0 - s))).astype(BF16), (back * a * s).astype(BF16)
+
+    for copy in dense:
+        copy.wait()
+    da, db = slopes(
+        contract_last(x_ref[...], weights[0, 0:ff, :]),
+        contract_last(x_ref[...], weights[1, 0:ff, :]),
+        contract_last(y_ref[...], weights[2, 0:ff, :]),
+    )
+    step = 512 if width % 512 == 0 else width
+    for low in range(0, width, step):
+        term = jnp.dot(da, weights[0, 0:ff, low:low + step], preferred_element_type=F32) + jnp.dot(
+            db, weights[1, 0:ff, low:low + step], preferred_element_type=F32
+        )
+        for j in range(chunks - n):
+            piece = term[j * chunk:min((j + 1) * chunk, rows)]
+            if piece.shape[0] < chunk:
+                piece = jnp.concatenate(
+                    [piece, jnp.zeros((chunk - piece.shape[0], step), F32)], axis=0
+                )
+            out[n + j, :, low:low + step] = piece.astype(BF16)
+    for copy in expert:
+        copy.start()
+
+    @pl.loop(n, chunks)
+    def _(i):
+        for e in range(p.ep):
+            sum_core(e, i).start()
+
+    @pl.loop(1, n)
+    def _(k):
+        forward(k)
+
+    pass_on(p.ctx_from(n - 1))
+    keep().wait()
+
+    @pl.loop(1, n)
+    def _(k):
+        @pl.when(p.c + k < n)
+        def _():
+            keys_to(p.c + k).start()
+
+        @pl.when(p.c - k >= 0)
+        def _():
+            queries_to(p.c - k).start()
+
+    for k in range(n):
+        src = p.ctx_from(k)
+        for e in range(p.ep):
+            from_core(e, src).wait_recv()
+        x_in[k * capacity:(k + 1) * capacity, :] = got[src, 0:capacity, :]
+        y_in[k * capacity:(k + 1) * capacity, :] = got[src, capacity:2 * capacity, :]
+
+    for copy in expert:
+        copy.wait()
+    for low in range(0, eh, 256):
+        high = min(low + 256, eh)
+        ga, gb = slopes(
+            contract_last(x_in[...], weights[0, low:high, :]),
+            contract_last(x_in[...], weights[1, low:high, :]),
+            contract_last(y_in[...], weights[2, low:high, :]),
+        )
+        grad_a[:, low:high] = ga
+        grad_b[:, low:high] = gb
+        if low == 0:
+
+            @pl.loop(n, chunks)
+            def _(i):
+                for b in range(1, p.ep):
+                    pass_sum(b, i)
+
+    def chunk_of(k):
+        return lax.rem(p.c + k + 1, n)
+
+    for mine in (False, True):
+        for b in list(range(1, p.ep)) + [0]:
+            t, e = (p.t if mine else 1 - p.t), p.ep_peer(b)
+            value = jnp.dot(grad_a[...], weights[0, 0:eh, cols(t, e)], preferred_element_type=F32) + jnp.dot(
+                grad_b[...], weights[1, 0:eh, cols(t, e)], preferred_element_type=F32
+            )
+            for k in range(n):
+                piece = jnp.concatenate(
+                    [value[k * capacity:(k + 1) * capacity], jnp.zeros((chunk - capacity, part), F32)],
+                    axis=0,
+                )
+                out[p.ctx_from(k), :, cols(t, e)] = piece.astype(BF16)
+            if not mine:
+
+                @pl.loop(0, n)
+                def _(k):
+                    sum_core(e, chunk_of(k)).start()
+
+            elif b:
+
+                @pl.loop(0, n)
+                def _(k):
+                    pass_sum(b, chunk_of(k))
+
+    @pl.loop(0, n - 1)
+    def _(k):
+        i = chunk_of(k)
+        fin_ref[i] = total(i).astype(BF16)
+        home(i).start()
+
+    back_ref[p.c] = total(p.c).astype(BF16)
+
+    @pl.loop(n, chunks)
+    def _(i):
+        dense_ref[i - n] = total(i)
+
+    keep_kvq().wait()
+
+    @pl.loop(1, n)
+    def _(k):
+        @pl.when(p.c + k < n)
+        def _():
+            keys_to(p.c + k).wait_send()
+            queries_from(p.c + k).wait_recv()
+
+        @pl.when(p.c - k >= 0)
+        def _():
+            queries_to(p.c - k).wait_send()
+            keys_from(p.c - k).wait_recv()
+
+        across(k).wait_send()
+        home(p.ctx_peer(k)).wait_send()
+        home_from(p.ctx_from(k)).wait_recv()
+
+    @pl.loop(0, n)
+    def _(src):
+        for e in range(p.ep):
+            to_core(e, src).wait_send()
+        for b in range(1, p.ep):
+            to_ep(b, src).wait_send()
+
+    @pl.loop(0, chunks)
+    def _(i):
+        for e in range(p.ep):
+            sum_core(e, i).wait_send()
+        for b in range(1, p.ep):
+            sum_ep(b, i).wait_send()
+
+
 def group_kernel(dims, own_ref, all_ref, send2, recv2, send3, recv3):
     p = Place(*dims)
     p.greet(False, True)
@@ -356,12 +647,10 @@
     seq = n * rows
     scale = HEAD_DIM ** (-0.5)
 
-    def across(k):
-        d = p.ctx_peer(k)
+    def across(d):
         return remote(g_ref, g_all.at[p.c], send1.at[d], recv1.at[p.c], p.at(c=d))
 
-    def across_stats(k):
-        d = p.ctx_peer(k)
+    def across_stats(d):
         return remote(mine, stats.at[p.c], send2.at[d], recv2.at[p.c], p.at(c=d))
 
     def arrive(src):
@@ -372,10 +661,16 @@
 
     @pl.loop(1, n)
     def _(k):
-        across(k).start()
+        @pl.when(p.c - k >= 0)
+        def _():
+            across(p.c - k).start()
 
     g_all[p.c] = g_ref[...]
     mine[...] = jnp.zeros_like(mine)
+    token = lax.broadcasted_iota(jnp.int32, (seq, HEAD_DIM), 0)
+    early = token < (p.c + 1) * rows
+    late = token >= p.c * rows
+    nothing = jnp.zeros((seq, HEAD_DIM), BF16)
     query_at = p.c * rows + lax.broadcasted_iota(jnp.int32, (rows, seq), 0)
     key_at = lax.broadcasted_iota(jnp.int32, (rows, seq), 1)
     allowed = key_at <= query_at
@@ -383,6 +678,8 @@
         cols = pl.ds(h * HEAD_DIM, HEAD_DIM)
         keys = kvq_ref[:, :, h * HEAD_DIM:(h + 1) * HEAD_DIM].reshape(seq, HEAD_DIM)
         values = kvq_ref[:, :, width + h * HEAD_DIM:width + (h + 1) * HEAD_DIM].reshape(seq, HEAD_DIM)
+        keys = jnp.where(early, keys, nothing)
+        values = jnp.where(early, values, nothing)
         q = kvq_ref[p.c, :, pl.ds(2 * width + h * HEAD_DIM, HEAD_DIM)]
         scores = jnp.where(allowed, contract_last(q, keys) * scale, NEG_FILL)
         top = jnp.max(scores, axis=1, keepdims=True)
@@ -399,14 +696,18 @@
 
     @pl.loop(1, n)
     def _(k):
-        across_stats(k).start()
+        @pl.when(p.c - k >= 0)
+        def _():
+            across_stats(p.c - k).start()
 
     stats[p.c] = mine[...]
 
     @pl.loop(1, n)
     def _(k):
-        arrive(p.ctx_from(k)).wait_recv()
-        arrive_stats(p.ctx_from(k)).wait_recv()
+        @pl.when(p.c + k < n)
+        def _():
+            arrive(p.c + k).wait_recv()
+            arrive_stats(p.c + k).wait_recv()
 
     key_at = p.c * rows + lax.broadcasted_iota(jnp.int32, (rows, seq), 0)
     query_at = lax.broadcasted_iota(jnp.int32, (rows, seq), 1)
@@ -417,20 +718,26 @@
             seq, HEAD_DIM
         )
         upstream = g_all[:, :, h * HEAD_DIM:(h + 1) * HEAD_DIM].reshape(seq, HEAD_DIM)
+        queries = jnp.where(late, queries, nothing)
+        upstream = jnp.where(late, upstream, nothing)
         keys = kvq_ref[p.c, :, pl.ds(h * HEAD_DIM, HEAD_DIM)]
         values = kvq_ref[p.c, :, pl.ds(width + h * HEAD_DIM, HEAD_DIM)]
         delta = jnp.concatenate([stats[s, h:h + 1, :] for s in range(n)], axis=1)
         log_norm = jnp.concatenate([stats[s, heads + h:heads + h + 1, :] for s in range(n)], axis=1)
         scores = contract_last(keys, queries) * scale
         probs = jnp.where(allowed, jnp.exp(jnp.where(allowed, scores - log_norm, 0.0)), 0.0)
-        grad_scores = (probs * (contract_last(values, upstream) - delta)).astype(BF16)
+        grad_scores = jnp.where(
+            allowed, probs * (contract_last(values, upstream) - delta), 0.0
+        ).astype(BF16)
         dv_ref[:, cols] = jnp.dot(probs.astype(BF16), upstream, preferred_element_type=F32).astype(BF16)
         dk_ref[:, cols] = (jnp.dot(grad_scores, queries, preferred_element_type=F32) * scale).astype(BF16)
 
     @pl.loop(1, n)
     def _(k):
-        across(k).wait_send()
-        across_stats(k).wait_send()
+        @pl.when(p.c - k >= 0)
+        def _():
+            across(p.c - k).wait_send()
+            across_stats(p.c - k).wait_send()
 
 
 def params(collective_id, grid=False):
@@ -442,50 +749,16 @@
     )
 
 
-def body(
-    dims, hidden, grad_out, gain, dense_gate, dense_up, dense_down, expert_gate, expert_up, expert_down,
-    out_proj, queries, keys, values, route_ids, route_weights
+def plain_route(
+    dims, sizes, send_rows, mixed_in, grad_out, dense_gate, dense_up, dense_down,
+    expert_gate, expert_up, expert_down, kvq
 ):
     n, tp, ep = dims
     group = tp * ep
-    rows, width = hidden.shape
+    capacity, pair, chunk = sizes
+    rows, width = mixed_in.shape
     part = width // group
-    picks = route_ids.shape[1]
-    capacity = 5 * rows // (2 * n)
-    pair = round_up(2 * capacity, 16)
-    chunk = round_up(capacity, 16)
     sem = pltpu.SemaphoreType.DMA
-    at = lax.axis_index("tp") * ep + lax.axis_index("ep")
-
-    hidden_f = hidden.astype(F32)
-    inverse = lax.rsqrt(jnp.mean(hidden_f * hidden_f, axis=1, keepdims=True) + EPSILON)
-    normed = hidden_f * inverse
-    mixed_in = (normed * gain).astype(BF16)
-
-    flat_ids = route_ids.reshape(-1)
-    hits = (flat_ids[:, None] == lax.iota(jnp.int32, n)[None, :]).astype(BF16)
-    order = lax.iota(jnp.int32, picks * rows)
-    before = (order[None, :] < order[:, None]).astype(BF16)
-    earlier = jnp.dot(before, hits, preferred_element_type=F32)
-    slots = jnp.sum(earlier * hits.astype(F32), axis=1).astype(jnp.int32)
-    slots = slots.reshape(rows, picks)
-    pair_at = (route_ids * pair + slots).T
-    home_at = route_ids * chunk + slots
-    places = lax.iota(jnp.int32, n * pair)[:, None]
-    own_in = lax.dynamic_slice(mixed_in, (0, at * part), (rows, part))
-    own_out = lax.dynamic_slice(grad_out, (0, at * part), (rows, part))
-    pick_in = sum((places == pair_at[k][None, :]).astype(BF16) for k in range(picks))
-    pick_out = [(places == pair_at[k][None, :] + capacity) for k in range(picks)]
-    weight_of = sum(
-        jnp.sum(jnp.where(pick_out[k], route_weights[:, k][None, :], 0.0), axis=1, keepdims=True)
-        for k in range(picks)
-    )
-    pick_out = sum(hit.astype(BF16) for hit in pick_out)
-    send_rows = (
-        jnp.dot(pick_in, own_in, preferred_element_type=F32)
-        + jnp.dot(pick_out, own_out, preferred_element_type=F32) * weight_of
-    ).astype(BF16).reshape(n, pair, part)
-
     ff = dense_gate.shape[0]
     ff_tile = tile_of(ff, 320)
     weight_spec = pl.BlockSpec((ff_tile, width), lambda i: (i, 0))
@@ -510,8 +783,7 @@
     def joined(low):
         return arrived[:, :, low:low + capacity].transpose(1, 2, 0, 3).reshape(n * capacity, width)
 
-    kvq = jnp.concatenate([keys, values, queries], axis=1)
-    head_width = queries.shape[1]
+    head_width = kvq.shape[1] // 3
     eh = expert_gate.shape[1]
     eh_tile = tile_of(eh, 320)
     weight_spec = pl.BlockSpec((1, eh_tile, width), lambda i: (0, i, 0))
@@ -558,12 +830,110 @@
         compiler_params=params(3),
         name="return_rows",
     )(parts)
+    return returned, dense_sum, kvq_all
+
+
+def fused_route(
+    dims, sizes, send_rows, mixed_in, grad_out, dense_gate, dense_up, dense_down,
+    expert_gate, expert_up, expert_down, kvq
+):
+    n, tp, ep = dims
+    capacity, pair, chunk = sizes
+    rows, width = mixed_in.shape
+    part = width // (tp * ep)
+    sem = pltpu.SemaphoreType.DMA
+    eh = expert_gate.shape[1]
+    dense_chunks = -(-rows // chunk)
+    chunks = n + dense_chunks
+    return pl.pallas_call(
+        functools.partial(experts_kernel, dims, capacity),
+        out_shape=(
+            jax.ShapeDtypeStruct((n, chunk, part), BF16),
+            jax.ShapeDtypeStruct((dense_chunks, chunk, part), F32),
+            jax.ShapeDtypeStruct((n,) + kvq.shape, BF16),
+        ),
+        in_specs=[ANY, WHOLE, WHOLE] + [ANY] * 7,
+        out_specs=(WHOLE, WHOLE, ANY),
+        scratch_shapes=[
+            pltpu.VMEM((n, pair, width), BF16),
+            pltpu.VMEM((n * capacity, width), BF16),
+            pltpu.VMEM((n * capacity, width), BF16),
+            pltpu.VMEM((3, max(eh, dense_gate.shape[0]), width), BF16),
+            pltpu.VMEM((n * capacity, eh), BF16),
+            pltpu.VMEM((n * capacity, eh), BF16),
+            pltpu.VMEM((chunks, chunk, width), BF16),
+            pltpu.VMEM((ep, chunks, chunk, part), BF16),
+            pltpu.VMEM((max(ep - 1, 1), chunks, chunk, part), BF16),
+            pltpu.VMEM((max(ep - 1, 1), chunks, chunk, part), BF16),
+            pltpu.VMEM((n, chunk, part), BF16),
+        ]
+        + [sem((n,))] * 2 + [sem((ep, n))] * 4 + [sem((ep, chunks))] * 4 + [sem((n,))] * 6
+        + [sem((3,)), sem((2,))],
+        compiler_params=params(6),
+        name="experts",
+    )(
+        send_rows, mixed_in, grad_out, dense_gate, dense_up, dense_down,
+        expert_gate, expert_up, expert_down, kvq
+    )
+
+
+def body(
+    dims, hidden, grad_out, gain, dense_gate, dense_up, dense_down, expert_gate, expert_up, expert_down,
+    out_proj, queries, keys, values, route_ids, route_weights
+):
+    n, tp, ep = dims
+    group = tp * ep
+    rows, width = hidden.shape
+    part = width // group
+    picks = route_ids.shape[1]
+    capacity = 5 * rows // (2 * n)
+    pair = round_up(2 * capacity, 16)
+    chunk = round_up(capacity, 16)
+    sem = pltpu.SemaphoreType.DMA
+    at = lax.axis_index("tp") * ep + lax.axis_index("ep")
+
+    hidden_f = hidden.astype(F32)
+    inverse = lax.rsqrt(jnp.mean(hidden_f * hidden_f, axis=1, keepdims=True) + EPSILON)
+    normed = hidden_f * inverse
+    mixed_in = (normed * gain).astype(BF16)
+
+    flat_ids = route_ids.reshape(-1)
+    hits = (flat_ids[:, None] == lax.iota(jnp.int32, n)[None, :]).astype(BF16)
+    order = lax.iota(jnp.int32, picks * rows)
+    before = (order[None, :] < order[:, None]).astype(BF16)
+    earlier = jnp.dot(before, hits, preferred_element_type=F32)
+    slots = jnp.sum(earlier * hits.astype(F32), axis=1).astype(jnp.int32)
+    slots = slots.reshape(rows, picks)
+    pair_at = (route_ids * pair + slots).T
+    home_at = route_ids * chunk + slots
+    places = lax.iota(jnp.int32, n * pair)[:, None]
+    own_in = lax.dynamic_slice(mixed_in, (0, at * part), (rows, part))
+    own_out = lax.dynamic_slice(grad_out, (0, at * part), (rows, part))
+    pick_in = sum((places == pair_at[k][None, :]).astype(BF16) for k in range(picks))
+    pick_out = [(places == pair_at[k][None, :] + capacity) for k in range(picks)]
+    weight_of = sum(
+        jnp.sum(jnp.where(pick_out[k], route_weights[:, k][None, :], 0.0), axis=1, keepdims=True)
+        for k in range(picks)
+    )
+    pick_out = sum(hit.astype(BF16) for hit in pick_out)
+    send_rows = (
+        jnp.dot(pick_in, own_in, preferred_element_type=F32)
+        + jnp.dot(pick_out, own_out, preferred_element_type=F32) * weight_of
+    ).astype(BF16).reshape(n, pair, part)
+
+    kvq = jnp.concatenate([keys, values, queries], axis=1)
+    head_width = queries.shape[1]
+    route = fused_route if part % 128 == 0 else plain_route
+    returned, dense_sum, kvq_all = route(
+        dims, (capacity, pair, chunk), send_rows, mixed_in, grad_out, dense_gate, dense_up, dense_down,
+        expert_gate, expert_up, expert_down, kvq
+    )
 
     home_places = lax.iota(jnp.int32, n * chunk)[None, :]
     take = sum((home_places == home_at[:, k:k + 1]).astype(BF16) for k in range(picks))
     own_total = (
         jnp.dot(take, returned.reshape(n * chunk, part), preferred_element_type=F32)
-        + dense_sum.reshape(dense_chunks * chunk, part)[:rows]
+        + dense_sum.reshape(-1, part)[:rows]
     ).astype(BF16)
     total_grad = pl.pallas_call(
         functools.partial(group_kernel, dims),

time: 202 us -> 138 us (0.68)
  Pallas kernels: 161 us -> 115 us
  local copies, waits for them, and re-layouts: 23.6 us -> 7.22 us
    pallas_call x3 -> x1, Pallas kernels: 130 us -> 79.7 us  [fused_route(): pl.pallas_call(functools.partial(experts_kernel, dims, capacity), out_sha...]
    unnamed x28 -> x16, local copies, waits for them, and re-layouts: 13.3 us -> 5.93 us
    reshape x3 -> x0, local copies, waits for them, and re-layouts: 6.13 us -> none  [the longest x2 6.05 us: body(): expert_part.reshape(n, capacity, group, part)]
    pallas_call x1, Pallas kernels: 20.1 us -> 24.4 us  [body(): pl.pallas_call(functools.partial(attention_kernel, dims), out_shape=(grad...]
    slice x1 -> x0, local copies, waits for them, and re-layouts: 2.72 us -> none  [joined(): arrived[:, :, low:low + capacity].transpose(1, 2, 0, 3)]
where the time goes in v2:
time: 138 us; the launch traced here: 137 us
  Pallas kernels  115 us (83%)
  other arithmetic  7.59 us (6%)
  local copies, waits for them, and re-layouts  7.22 us (5%)
  matrix products  6.69 us (5%)
    pallas_call x1, Pallas kernels, fused_route(): pl.pallas_call(functools.partial(experts_kernel, dims, capacity), out_sha...  79.7 us
    pallas_call x1, Pallas kernels, body(): pl.pallas_call(functools.partial(attention_kernel, dims), out_shape=(grad...  24.4 us
    pallas_call x1, Pallas kernels, body(): pl.pallas_call(functools.partial(group_kernel, dims), out_shape=jax.Shape...  10.8 us
    unnamed x16, local copies, waits for them, and re-layouts  5.93 us

profile of v2, /device:TPU:0, one launch (start us, length us, event | category | flops | bytes accessed | tf_op | source)
XLA Modules:
  0.0 137.2 jit_solution(8698211895175293181)
XLA Ops:
  0.6 0.0 copy-start
  0.6 0.0 copy-start.1
  0.7 1.6 %fusion.9 = f32[128]{0:T(128)S(1)} fusion(bf16[128,3584]{1,0:T(8,128)(2,1)} %param.15), kind=kLoop, calls=%fused_computation.12 | loop fusion | flops 1376128 | bytes 918016 | tf_op jit(solution)/shard_map/reduce_sum | solution.py:896
  2.3 0.8 slice_bitcast_fusion
  3.0 0.8 copy.38
  3.8 0.1 eq.106
  4.0 0.2 fusion.11
  4.2 0.1 convert_element_type.70
  4.3 0.1 copy.39
  4.4 0.7 multiply_add_fusion
  5.1 0.2 select_reduce_fusion
  5.4 1.6 %pad_maximum_fusion.kvq_ref = bf16[128,768]{1,0:T(8,128)(2,1)} fusion(bf16[128,256]{1,0:T(8,128)(2,1)} %param.25, bf16[128,256]{1,0:T(8,128)(2,1)} %param.27, bf16[128,256]{1,0:T(8,128)(2,1)} %param.26), kind=kLoop, calls=%fused_computation.33 | loop fusion | flops 589824 | bytes 393216 | tf_op jit(solution)/shard_map/concatenate | solution.py:924
  6.9 0.0 copy-done.1
  7.0 1.0 fusion.3.x_ref
  8.0 0.0 copy-start.3
  8.0 0.5 fusion.17
  8.4 2.4 %add_convert_fusion = bf16[640,896]{1,0:T(8,128)(2,1)} fusion(f32[640,896]{1,0:T(8,128)S(1)} %fusion.17, f32[640]{0:T(1024)S(1)} %add.67, bf16[128,3584]{1,0:T(8,128)(2,1)} %y_ref.1, s32[]{:T(128)S(6)} %select_n.11, s32[128]{0:T(128)S(1)} %get-tuple-element.20, s32[128]{0:T(128)S(1)} %get-tuple-element.21), kind=kOutput, calls=%fused_computation | convolution fusion | flops 149176320 | bytes 3673604 | tf_op jit(solution)/shard_map/dot_general | solution.py:921
  10.8 0.0 copy-done.3
  10.9 79.7 %experts.1 = (bf16[8,48,896]{2,1,0:T(8,128)(2,1)}, f32[3,48,896]{2,1,0:T(8,128)}, bf16[8,128,768]{2,1,0:T(8,128)(2,1)}) custom-call(bf16[8,80,896]{2,1,0:T(8,128)(2,1)} %bitcast.33, bf16[128,3584]{1,0:T(8,128)(2,1)} %copy-done.3, bf16[128,3584]{1,0:T(8,128)(2,1)} %y_ref.1, bf16[608,3584]{1,0:T(8,128)(2,1)} %dense_gate.1, bf16[608,3584]{1,0:T(8,128)(2,1)} %dense_up.1, ...), custom_call_target="tpu_custom_call" | custom-call | tf_op jit(solution)/shard_map/experts/pallas_call | solution.py:848
  90.6 2.3 %fusion.10.own_ref = bf16[128,896]{1,0:T(8,128)(2,1)} fusion(bf16[384,896]{1,0:T(8,128)(2,1)} %bitcast.34, f32[144,896]{1,0:T(8,128)} %bitcast.35, s32[128]{0:T(128)S(1)} %get-tuple-element.19, s32[128]{0:T(128)S(1)} %get-tuple-element.18), kind=kOutput, calls=%fused_computation.15 | convolution fusion | flops 88702976 | bytes 1377280 | tf_op jit(solution)/shard_map/dot_general | solution.py:935
  92.9 10.8 %group_gather.1 = bf16[2,2,128,896]{3,2,1,0:T(8,128)(2,1)} custom-call(bf16[128,896]{1,0:T(8,128)(2,1)} %fusion.10.own_ref), custom_call_target="tpu_custom_call" | custom-call | tf_op jit(solution)/shard_map/group_gather/pallas_call | solution.py:938
  103.7 1.3 convert_bitcast_fusion
  105.0 0.0 copy-start.5
  105.0 0.2 copy.42
  105.2 0.0 copy-start.2
  105.2 0.5 copy-done.5
  105.7 0.5 fusion.4
  106.2 0.2 copy-done.2
  106.4 0.6 fusion.8
  107.0 0.0 copy-done
  107.0 0.0 copy-start.4
  107.1 1.3 convolution_convert_fusion.g_ref
  108.4 24.4 %attention_grads.1 = (bf16[128,256]{1,0:T(8,128)(2,1)}, bf16[128,256]{1,0:T(8,128)(2,1)}, bf16[128,256]{1,0:T(8,128)(2,1)}) custom-call(bf16[128,256]{1,0:T(8,128)(2,1)} %convolution_convert_fusion.g_ref, bf16[8,128,768]{2,1,0:T(8,128)(2,1)} %get-tuple-element.12.kvq_ref), custom_call_target="tpu_custom_call" | custom-call | tf_op jit(solution)/shard_map/attention_grads/pallas_call | solution.py:958
  132.8 0.0 copy-done.4
  132.8 1.5 %copy.46 = bf16[128,256]{1,0:T(8,128)(2,1)} copy(bf16[128,256]{1,0:T(8,128)(2,1)} %get-tuple-element.33) | data formatting | bytes 131072
  134.3 1.5 %copy.47 = bf16[128,256]{1,0:T(8,128)(2,1)} copy(bf16[128,256]{1,0:T(8,128)(2,1)} %get-tuple-element.34) | data formatting | bytes 131072
  135.8 1.5 %copy.48 = bf16[128,256]{1,0:T(8,128)(2,1)} copy(bf16[128,256]{1,0:T(8,128)(2,1)} %get-tuple-element.35) | data formatting | bytes 131072
  (6 shorter events, 0.0 us)
Async XLA Ops:
  0.6 106.4 %copy-start = (bf16[256,3584]{1,0:T(8,128)(2,1)S(1)}, bf16[256,3584]{1,0:T(8,128)(2,1)}, u32[]{:S(2)}) copy-start(bf16[256,3584]{1,0:T(8,128)(2,1)} %param.24) | copy-start | bytes 5505028
  0.6 6.3 %copy-start.1 = (bf16[128,3584]{1,0:T(8,128)(2,1)S(1)}, bf16[128,3584]{1,0:T(8,128)(2,1)}, u32[]{:S(2)}) copy-start(bf16[128,3584]{1,0:T(8,128)(2,1)} %param.15) | copy-start | bytes 2752516
  8.0 2.9 %copy-start.3 = (bf16[128,3584]{1,0:T(8,128)(2,1)}, bf16[128,3584]{1,0:T(8,128)(2,1)S(1)}, u32[]{:S(2)}) copy-start(bf16[128,3584]{1,0:T(8,128)(2,1)S(1)} %fusion.3.x_ref) | copy-start | bytes 2752516
  105.0 0.7 copy-start.5
  105.2 1.2 copy-start.2
  107.0 25.8 %copy-start.4 = (bf16[128,3584]{1,0:T(8,128)(2,1)}, bf16[128,3584]{1,0:T(8,128)(2,1)S(1)}, u32[]{:S(2)}) copy-start(bf16[128,3584]{1,0:T(8,128)(2,1)S(1)} %fusion.8) | copy-start | bytes 2752516

commit v3 on v2

--- a/solution.py
+++ b/solution.py
@@ -313,11 +313,13 @@
 
 
 def experts_kernel(
-    dims, capacity, rows_ref, x_ref, y_ref, dense_gate, dense_up, dense_down,
-    expert_gate, expert_up, expert_down, kvq_ref, back_ref, dense_ref, all_ref,
-    got, x_in, y_in, weights, grad_a, grad_b, out, core_buf, ep_out, ep_in, fin_ref,
+    dims, capacity, rows_ref, x_ref, y_ref, hidden_ref, gain_ref, home_ref, proj_ref,
+    k_ref, v_ref, q_ref, dense_gate, dense_up, dense_down, expert_gate, expert_up, expert_down,
+    hidden_out, heads_out,
+    got, x_in, y_in, weights, grad_a, grad_b, out, core_buf, ep_out, ep_in, fin_ref, back_ref,
+    dense_ref, joint, k_all, v_all, q_all, g_all, probs_ref, turned_ref, norms, deltas, my_norms, my_deltas,
     send1, recv1, send2, recv2, send3, recv3, send4, recv4, send5, recv5, send6, recv6,
-    send7, recv7, send8, recv8, loads, local
+    send7, recv7, send8, recv8, sent, landed, loads, local
 ):
     p = Place(*dims)
     n = p.n
@@ -325,7 +327,10 @@
     rows, width = x_ref.shape
     ff, eh = dense_gate.shape[0], expert_gate.shape[1]
     chunks, chunk = out.shape[0], out.shape[1]
-    head_width = kvq_ref.shape[1] // 3
+    head_width = k_ref.shape[1]
+    heads = head_width // HEAD_DIM
+    seq = n * rows
+    scale = HEAD_DIM ** (-0.5)
 
     def cols(t, e):
         return pl.ds(pl.multiple_of((t * p.ep + e) * part, 128), part)
@@ -371,13 +376,15 @@
             from_ep(b, src).wait_recv()
             to_core(p.ep_from(b), src).start()
 
-    def forward(k):
-        src = p.ctx_from(k)
+    def forward(at):
+        src = p.ctx_from(shifts[at])
         arrive(src).wait_recv()
+        if at + 3 < n - 1:
+            across(shifts[at + 3]).start()
         for b in range(1, p.ep):
             to_ep(b, src).start()
         to_core(p.e, src).start()
-        pass_on(p.ctx_from(k - 1))
+        pass_on(p.ctx_from(shifts[at - 1] if at else 0))
 
     def sum_core(e, i):
         return remote(
@@ -410,32 +417,44 @@
     def home_from(src):
         return remote(fin_ref.at[src], back_ref.at[src], send6.at[src], recv6.at[src], p.at(c=src))
 
-    def keys_to(d):
-        at = pl.ds(0, 2 * head_width)
-        return remote(
-            kvq_ref.at[:, at], all_ref.at[p.c, :, at], send7.at[d], recv7.at[p.c], p.at(c=d)
-        )
-
-    def keys_from(src):
-        at = pl.ds(0, 2 * head_width)
-        return remote(
-            kvq_ref.at[:, at], all_ref.at[src, :, at], send7.at[src], recv7.at[src], p.at(c=src)
-        )
-
-    def queries_to(d):
-        at = pl.ds(2 * head_width, head_width)
-        return remote(
-            kvq_ref.at[:, at], all_ref.at[p.c, :, at], send8.at[d], recv8.at[p.c], p.at(c=d)
-        )
-
-    def queries_from(src):
-        at = pl.ds(2 * head_width, head_width)
-        return remote(
-            kvq_ref.at[:, at], all_ref.at[src, :, at], send8.at[src], recv8.at[src], p.at(c=src)
-        )
-
-    def keep_kvq():
-        return pltpu.make_async_copy(kvq_ref, all_ref.at[p.c], local.at[1])
+    shared = [
+        (k_ref, k_all, 1), (v_ref, v_all, 1), (q_ref, q_all, -1),
+        (my_norms, norms, -1), (g_all.at[p.c], g_all, -1), (my_deltas, deltas, -1),
+    ]
+
+    def share(j, d):
+        src, dst, _ = shared[j]
+        return remote(src, dst.at[p.c], sent.at[j, d], landed.at[j, p.c], p.at(c=d))
+
+    def shared_from(j, src):
+        block, dst, _ = shared[j]
+        return remote(block, dst.at[src], sent.at[j, src], landed.at[j, src], p.at(c=src))
+
+    def each(items, onward, act):
+        @pl.loop(1, n)
+        def _(k):
+            for j in items:
+                up = (shared[j][2] > 0) == onward
+                peer = p.c + k if up else p.c - k
+
+                @pl.when(peer < n if up else peer >= 0)
+                def _():
+                    act(j, peer)
+
+    def share_all(*items):
+        each(items, True, lambda j, d: share(j, d).start())
+
+    def wait_all(*items):
+        each(items, False, lambda j, src: shared_from(j, src).wait_recv())
+
+    def joint_ep(b, mine):
+        e = p.e if mine else p.ep_from(b)
+        slot = joint.at[:, cols(p.t, e)]
+        return remote(slot, slot, send7.at[b], recv7.at[b], p.at(e=p.ep_peer(b)))
+
+    def joint_core(e, mine):
+        slot = joint.at[:, cols(p.t if mine else 1 - p.t, e)]
+        return remote(slot, slot, send8.at[e], recv8.at[e], p.at(t=1 - p.t))
 
     def load(j, ref, size):
         return pltpu.make_async_copy(ref, weights.at[j, pl.ds(0, size)], loads.at[j])
@@ -446,17 +465,20 @@
     ]
     for copy in dense:
         copy.start()
+    for ref in (k_all, v_all, q_all, g_all, norms, deltas, my_norms, my_deltas):
+        ref[...] = jnp.zeros_like(ref)
     p.greet(True, True)
-
-    @pl.loop(1, n)
-    def _(k):
+    shifts = sorted(range(1, n), key=lambda k: abs(2 * k - n))
+
+    for k in shifts[:3]:
         across(k).start()
-
     for b in range(1, p.ep):
         to_ep(b, p.c, True).start()
     to_core(p.e, p.c, True).start()
     keep().start()
-    keep_kvq().start()
+    k_all[p.c] = k_ref[...]
+    v_all[p.c] = v_ref[...]
+    q_all[p.c] = q_ref[...]
 
     def slopes(a, b, back):
         s = jax.nn.sigmoid(a)
@@ -470,7 +492,11 @@
         contract_last(y_ref[...], weights[2, 0:ff, :]),
     )
     step = 512 if width % 512 == 0 else width
+    done = 0
     for low in range(0, width, step):
+        if low * 2 >= width * done and done < min(2, n - 1):
+            forward(done)
+            done += 1
         term = jnp.dot(da, weights[0, 0:ff, low:low + step], preferred_element_type=F32) + jnp.dot(
             db, weights[1, 0:ff, low:low + step], preferred_element_type=F32
         )
@@ -489,23 +515,12 @@
         for e in range(p.ep):
             sum_core(e, i).start()
 
-    @pl.loop(1, n)
-    def _(k):
-        forward(k)
-
-    pass_on(p.ctx_from(n - 1))
+    for at in range(done, n - 1):
+        forward(at)
+    pass_on(p.ctx_from(shifts[-1]))
     keep().wait()
 
-    @pl.loop(1, n)
-    def _(k):
-        @pl.when(p.c + k < n)
-        def _():
-            keys_to(p.c + k).start()
-
-        @pl.when(p.c - k >= 0)
-        def _():
-            queries_to(p.c - k).start()
-
+    share_all(0, 1, 2)
     for k in range(n):
         src = p.ctx_from(k)
         for e in range(p.ep):
@@ -566,27 +581,108 @@
 
     back_ref[p.c] = total(p.c).astype(BF16)
 
-    @pl.loop(n, chunks)
-    def _(i):
-        dense_ref[i - n] = total(i)
-
-    keep_kvq().wait()
+    for i in range(n, chunks):
+        dense_ref[(i - n) * chunk:(i - n + 1) * chunk, :] = total(i)
+
+    wait_all(0, 1)
+    query_at = p.c * rows + lax.broadcasted_iota(jnp.int32, (rows, seq), 0)
+    key_at = lax.broadcasted_iota(jnp.int32, (rows, seq), 1)
+    allowed = key_at <= query_at
+    heads_at = [slice(h * HEAD_DIM, (h + 1) * HEAD_DIM) for h in range(heads)]
+
+    def across_rows(column):
+        return jnp.transpose(jnp.broadcast_to(column, (rows, 128)))[0:1, :]
+
+    for h, at in enumerate(heads_at):
+        keys = k_all[:, :, at].reshape(seq, HEAD_DIM)
+        scores = jnp.where(allowed, contract_last(q_ref[:, at], keys) * scale, NEG_FILL)
+        top = jnp.max(scores, axis=1, keepdims=True)
+        powers = jnp.where(allowed, jnp.exp(scores - top), 0.0)
+        norm = jnp.sum(powers, axis=1, keepdims=True)
+        probs_ref[h] = powers / norm
+        my_norms[h:h + 1, :] = across_rows(top + jnp.log(norm))
+    share_all(3)
+    norms[p.c] = my_norms[...]
 
     @pl.loop(1, n)
     def _(k):
-        @pl.when(p.c + k < n)
-        def _():
-            keys_to(p.c + k).wait_send()
-            queries_from(p.c + k).wait_recv()
-
-        @pl.when(p.c - k >= 0)
-        def _():
-            queries_to(p.c - k).wait_send()
-            keys_from(p.c - k).wait_recv()
-
+        home_from(p.ctx_from(k)).wait_recv()
+
+    spots = lax.broadcasted_iota(jnp.int32, (rows, n * chunk), 1)
+    take = sum(
+        jnp.where(spots == home_ref[:, k:k + 1], 1.0, 0.0) for k in range(home_ref.shape[1])
+    ).astype(BF16)
+    joint[:, cols(p.t, p.e)] = (
+        jnp.dot(take, back_ref[...].reshape(n * chunk, part), preferred_element_type=F32)
+        + dense_ref[0:rows, :]
+    ).astype(BF16)
+    for b in range(1, p.ep):
+        joint_ep(b, True).start()
+    joint_core(p.e, True).start()
+
+    wait_all(2, 3)
+    turned_key = p.c * rows + lax.broadcasted_iota(jnp.int32, (rows, seq), 0)
+    turned_query = lax.broadcasted_iota(jnp.int32, (rows, seq), 1)
+    turned_allowed = turned_key <= turned_query
+    for h, at in enumerate(heads_at):
+        queries = q_all[:, :, at].reshape(seq, HEAD_DIM)
+        norm = jnp.concatenate([norms[s, h:h + 1, :] for s in range(n)], axis=1)
+        scores = contract_last(k_ref[:, at], queries) * scale
+        turned_ref[h] = jnp.where(
+            turned_allowed, jnp.exp(jnp.where(turned_allowed, scores - norm, 0.0)), 0.0
+        )
+
+    for b in range(1, p.ep):
+        joint_ep(b, False).wait_recv()
+        joint_core(p.ep_from(b), True).start()
+    hidden = hidden_ref[...].astype(F32)
+    inverse = lax.rsqrt(jnp.mean(hidden * hidden, axis=1, keepdims=True) + EPSILON)
+    for e in range(p.ep):
+        joint_core(e, False).wait_recv()
+    normed = hidden_ref[...].astype(F32) * inverse
+    scaled = joint[...].astype(F32) * gain_ref[...]
+    mean = jnp.mean(scaled * normed, axis=1, keepdims=True)
+    hidden_out[...] = (y_ref[...].astype(F32) + inverse * (scaled - normed * mean)).astype(BF16)
+    g_all[p.c] = contract_last(hidden_out[...], proj_ref[...]).astype(BF16)
+    share_all(4)
+
+    def grads(j, at, value):
+        heads_out[j, :, at] = value.astype(BF16)
+
+    g_own = g_all[p.c]
+    spread = []
+    for h, at in enumerate(heads_at):
+        values = v_all[:, :, at].reshape(seq, HEAD_DIM)
+        grad_probs = contract_last(g_own[:, at], values)
+        delta = jnp.sum(probs_ref[h] * grad_probs, axis=1, keepdims=True)
+        my_deltas[h:h + 1, :] = across_rows(delta)
+        spread.append((probs_ref[h] * (grad_probs - delta)).astype(BF16))
+    share_all(5)
+    deltas[p.c] = my_deltas[...]
+    for h, at in enumerate(heads_at):
+        keys = k_all[:, :, at].reshape(seq, HEAD_DIM)
+        grads(0, at, jnp.dot(spread[h], keys, preferred_element_type=F32) * scale)
+
+    wait_all(4, 5)
+    for h, at in enumerate(heads_at):
+        queries = q_all[:, :, at].reshape(seq, HEAD_DIM)
+        upstream = g_all[:, :, at].reshape(seq, HEAD_DIM)
+        delta = jnp.concatenate([deltas[s, h:h + 1, :] for s in range(n)], axis=1)
+        probs = turned_ref[h]
+        grad_scores = (probs * (contract_last(v_ref[:, at], upstream) - delta)).astype(BF16)
+        grads(1, at, jnp.dot(grad_scores, queries, preferred_element_type=F32) * scale)
+        grads(2, at, jnp.dot(probs.astype(BF16), upstream, preferred_element_type=F32))
+
+    each(range(len(shared)), True, lambda j, d: share(j, d).wait_send())
+    for b in range(1, p.ep):
+        joint_ep(b, True).wait_send()
+    for e in range(p.ep):
+        joint_core(e, True).wait_send()
+
+    @pl.loop(1, n)
+    def _(k):
         across(k).wait_send()
         home(p.ctx_peer(k)).wait_send()
-        home_from(p.ctx_from(k)).wait_recv()
 
     @pl.loop(0, n)
     def _(src):
@@ -740,11 +836,11 @@
             across_stats(p.c - k).wait_send()
 
 
-def params(collective_id, grid=False):
+def params(collective_id, grid=False, vmem=56):
     return pltpu.CompilerParams(
         collective_id=collective_id,
         has_side_effects=True,
-        vmem_limit_bytes=56 * 1024 * 1024,
+        vmem_limit_bytes=vmem * 1024 * 1024,
         **({"dimension_semantics": ("arbitrary",)} if grid else {}),
     )
 
@@ -834,26 +930,32 @@
 
 
 def fused_route(
-    dims, sizes, send_rows, mixed_in, grad_out, dense_gate, dense_up, dense_down,
-    expert_gate, expert_up, expert_down, kvq
+    dims, sizes, send_rows, mixed_in, grad_out, hidden, gain, home_at, out_proj, keys, values, queries,
+    dense_gate, dense_up, dense_down, expert_gate, expert_up, expert_down
 ):
     n, tp, ep = dims
     capacity, pair, chunk = sizes
     rows, width = mixed_in.shape
     part = width // (tp * ep)
+    head_width = keys.shape[1]
+    heads = head_width // HEAD_DIM
+    stat_rows = round_up(heads, 8)
     sem = pltpu.SemaphoreType.DMA
     eh = expert_gate.shape[1]
     dense_chunks = -(-rows // chunk)
     chunks = n + dense_chunks
+    blocks = pltpu.VMEM((n, rows, head_width), BF16)
+    squares = pltpu.VMEM((heads, rows, n * rows), F32)
+    stats = pltpu.VMEM((n, stat_rows, rows), F32)
+    own_stats = pltpu.VMEM((stat_rows, rows), F32)
     return pl.pallas_call(
         functools.partial(experts_kernel, dims, capacity),
         out_shape=(
-            jax.ShapeDtypeStruct((n, chunk, part), BF16),
-            jax.ShapeDtypeStruct((dense_chunks, chunk, part), F32),
-            jax.ShapeDtypeStruct((n,) + kvq.shape, BF16),
+            jax.ShapeDtypeStruct((rows, width), BF16),
+            jax.ShapeDtypeStruct((3, rows, head_width), BF16),
         ),
-        in_specs=[ANY, WHOLE, WHOLE] + [ANY] * 7,
-        out_specs=(WHOLE, WHOLE, ANY),
+        in_specs=[ANY] + [WHOLE] * 9 + [ANY] * 6,
+        out_specs=(WHOLE, WHOLE),
         scratch_shapes=[
             pltpu.VMEM((n, pair, width), BF16),
             pltpu.VMEM((n * capacity, width), BF16),
@@ -866,14 +968,19 @@
             pltpu.VMEM((max(ep - 1, 1), chunks, chunk, part), BF16),
             pltpu.VMEM((max(ep - 1, 1), chunks, chunk, part), BF16),
             pltpu.VMEM((n, chunk, part), BF16),
+            pltpu.VMEM((n, chunk, part), BF16),
+            pltpu.VMEM((dense_chunks * chunk, part), F32),
+            pltpu.VMEM((rows, width), BF16),
+            blocks, blocks, blocks, blocks, squares, squares, stats, stats, own_stats, own_stats,
         ]
-        + [sem((n,))] * 2 + [sem((ep, n))] * 4 + [sem((ep, chunks))] * 4 + [sem((n,))] * 6
-        + [sem((3,)), sem((2,))],
-        compiler_params=params(6),
-        name="experts",
+        + [sem((n,))] * 2 + [sem((ep, n))] * 4 + [sem((ep, chunks))] * 4 + [sem((n,))] * 2
+        + [sem((ep,))] * 4 + [sem((6, n))] * 2 + [sem((3,)), sem((1,))],
+        compiler_params=params(6, vmem=63),
+        name="layer_grads",
     )(
-        send_rows, mixed_in, grad_out, dense_gate, dense_up, dense_down,
-        expert_gate, expert_up, expert_down, kvq
+        send_rows, mixed_in, grad_out, hidden, gain.reshape(1, -1), home_at, out_proj,
+        keys, values, queries,
+        dense_gate, dense_up, dense_down, expert_gate, expert_up, expert_down
     )
 
 
@@ -921,10 +1028,16 @@
         + jnp.dot(pick_out, own_out, preferred_element_type=F32) * weight_of
     ).astype(BF16).reshape(n, pair, part)
 
+    if part % 128 == 0:
+        grad_hidden, head_grads = fused_route(
+            dims, (capacity, pair, chunk), send_rows, mixed_in, grad_out, hidden, gain, home_at, out_proj,
+            keys, values, queries, dense_gate, dense_up, dense_down, expert_gate, expert_up, expert_down
+        )
+        return (grad_hidden, head_grads[0], head_grads[1], head_grads[2])
+
     kvq = jnp.concatenate([keys, values, queries], axis=1)
     head_width = queries.shape[1]
-    route = fused_route if part % 128 == 0 else plain_route
-    returned, dense_sum, kvq_all = route(
+    returned, dense_sum, kvq_all = plain_route(
         dims, (capacity, pair, chunk), send_rows, mixed_in, grad_out, dense_gate, dense_up, dense_down,
         expert_gate, expert_up, expert_down, kvq
     )

time: 138 us -> 127 us (0.920)
  matrix products: 6.69 us -> 3.09 us
  other arithmetic: 7.59 us -> 4.53 us
  Pallas kernels: 115 us -> 112 us
    pallas_call x2 -> x0, Pallas kernels: 35.2 us -> none  [the longest x1 24.4 us: body(): pl.pallas_call(functools.partial(attention_kernel, dims), out_shape=(grad...]
    pallas_call x1, Pallas kernels: 79.7 us -> 112 us  [fused_route(): pl.pallas_call(functools.partial(experts_kernel, dims, capacity), out_sha...]
    dot_general x2 -> x0, matrix products: 3.6 us -> none  [the longest x1 2.26 us: body(): jnp.dot(take, returned.reshape(n * chunk, part), preferred_element_type=F32)]
    unnamed x16 -> x6, local copies, waits for them, and re-layouts: 5.93 us -> 2.96 us
    concatenate x1 -> x0, other arithmetic: 1.59 us -> none  [body(): kvq = jnp.concatenate([keys, values, queries], axis=1)]
    squeeze x0 -> x1, local copies, waits for them, and re-layouts: none -> 1.58 us  [body(): return (grad_hidden, head_grads[0], head_grads[1], head_grads[2])]
where the time goes in v3:
time: 127 us
  Pallas kernels  112 us (88%)
  local copies, waits for them, and re-layouts  6.35 us (5%)
  other arithmetic  4.53 us (4%)
  matrix products  3.09 us (2%)
    pallas_call x1, Pallas kernels, fused_route(): pl.pallas_call(functools.partial(experts_kernel, dims, capacity), out_sha...  112 us
    unnamed x6, local copies, waits for them, and re-layouts  2.96 us

profile of v3, /device:TPU:0, one launch (start us, length us, event | category | flops | bytes accessed | tf_op | source)
XLA Modules:
  0.0 126.9 jit_solution(1760767015056747951)
XLA Ops:
  0.6 0.8 copy.33
  1.4 0.1 eq.76
  1.6 0.2 fusion.3
  1.8 0.1 convert_element_type.38
  1.9 0.1 copy.34
  2.0 0.7 broadcast_multiply_fusion
  2.7 0.8 slice_bitcast_fusion.3
  3.4 0.2 select_reduce_fusion
  3.7 1.4 %fusion = f32[128]{0:T(128)S(1)} fusion(bf16[128,3584]{1,0:T(8,128)(2,1)} %hidden_ref.1), kind=kLoop, calls=%fused_computation.3 | loop fusion | flops 1376128 | bytes 918016 | tf_op jit(solution)/shard_map/reduce_sum | solution.py:1003
  5.2 1.5 %fusion.2.x_ref = bf16[128,3584]{1,0:T(8,128)(2,1)S(1)} fusion(bf16[128,3584]{1,0:T(8,128)(2,1)} %hidden_ref.1, f32[3584]{0:T(1024)} %param.17, f32[128]{0:T(128)S(1)} %add_rsqrt_fusion), kind=kLoop, calls=%fused_computation.5 | loop fusion | flops 1835008 | bytes 1849856 | tf_op jit(solution)/shard_map/convert_element_type | solution.py:1005
  6.6 0.0 copy-start
  6.7 0.5 fusion.9
  7.1 0.0 copy-start.1
  7.1 2.4 %add_convert_fusion = bf16[640,896]{1,0:T(8,128)(2,1)} fusion(f32[640,896]{1,0:T(8,128)S(1)} %fusion.9, f32[640]{0:T(1024)S(1)} %add.56, bf16[128,3584]{1,0:T(8,128)(2,1)} %y_ref.1, s32[]{:T(128)S(6)} %select_n.11, s32[128]{0:T(128)S(1)} %get-tuple-element.13, s32[128]{0:T(128)S(1)} %get-tuple-element.14), kind=kOutput, calls=%fused_computation | convolution fusion | flops 149176320 | bytes 3673604 | tf_op jit(solution)/shard_map/dot_general | solution.py:1028
  9.6 0.0 copy-done
  9.6 0.1 copy.35
  9.7 0.6 add.58.home_ref
  10.3 0.0 copy-done.1
  10.3 0.6 broadcast_in_dim.37.gain_ref
  10.9 112.2 %layer_grads.1 = (bf16[128,3584]{1,0:T(8,128)(2,1)}, bf16[3,128,256]{2,1,0:T(8,128)(2,1)}) custom-call(bf16[8,80,896]{2,1,0:T(8,128)(2,1)} %bitcast.21, bf16[128,3584]{1,0:T(8,128)(2,1)} %copy-done, bf16[128,3584]{1,0:T(8,128)(2,1)} %y_ref.1, bf16[128,3584]{1,0:T(8,128)(2,1)} %hidden_ref.1, f32[1,3584]{1,0:T(1,128)} %broadcast_in_dim.37.gain_ref, ...), custom_call_target="tpu_custom_call" | custom-call | tf_op jit(solution)/shard_map/layer_grads/pallas_call | solution.py:951
  123.2 1.6 %slice_bitcast_fusion = (bf16[128,256]{1,0:T(8,128)(2,1)}, bf16[128,256]{1,0:T(8,128)(2,1)}, bf16[128,256]{1,0:T(8,128)(2,1)}) fusion(bf16[3,128,256]{2,1,0:T(8,128)(2,1)} %get-tuple-element.7), kind=kLoop, calls=%fused_computation.28 | loop fusion | bytes 393216 | tf_op jit(solution)/shard_map/squeeze | solution.py:1036
  124.7 2.2 %copy.37 = bf16[128,3584]{1,0:T(8,128)(2,1)} copy(bf16[128,3584]{1,0:T(8,128)(2,1)} %get-tuple-element.25) | data formatting | bytes 1835008
  (4 shorter events, 0.0 us)
Async XLA Ops:
  6.6 2.9 %copy-start = (bf16[128,3584]{1,0:T(8,128)(2,1)}, bf16[128,3584]{1,0:T(8,128)(2,1)S(1)}, u32[]{:S(2)}) copy-start(bf16[128,3584]{1,0:T(8,128)(2,1)S(1)} %fusion.2.x_ref) | copy-start | bytes 2752516
  7.1 3.2 %copy-start.1 = (f32[3584]{0:T(1024)S(1)}, f32[3584]{0:T(1024)}, u32[]{:S(2)}) copy-start(f32[3584]{0:T(1024)} %param.17) | copy-start | bytes 43012
